TPU v7x, 32 devices: a whole 2x2x4 slice. The times are simulated.
32 devices in a mesh: rows: 4 (over z), lag: 8 (over y, x, core).
Axes of the slice: x: 2, y: 2, z: 4, core: 2. Of those that a mesh axis runs over, the one named last changes fastest.
Arguments:
- excitation: bfloat16 [4, 2048, 128], P(None, 'rows'), may hold values from -6 to 6
- pending: float32 [8, 2048, 128], P('lag', 'rows'), may hold values from -6 to 6
- inverse: float32 [16, 128, 128], P('rows'), may hold values from -0.5 to 0.5
- interaction: bfloat16 [3072, 128, 128], P(('rows', 'lag')), may hold values from -0.0390625 to 0.0390625
- slot_row: int32 [3072], P(('rows', 'lag')), may hold values from 0 to 3
- slot_owner: int32 [3072], P(('rows', 'lag')), may hold values from 0 to 3
- slot_pos: int32 [3072], P(('rows', 'lag')), may hold values from 0 to 1
- needed: int32 [32, 4, 2], P(('rows', 'lag')), may hold values from 0 to 3
- block_count: int32 [4, 8], P('rows', 'lag'), may hold values from 6 to 96, as said below
Outputs:
- currents: bfloat16 [4, 2048, 128], P(None, 'rows')
- carried: float32 [8, 2048, 128], P('lag', 'rows')
Inputs may be any that keep to these rules, and one draw needn't show every extreme that they name: `block_count`: every row owner and lag has at least 6 live slots, and some row owner and lag has all 96 live.
All inputs are finite; a program needn't handle non-finite values.
Results may differ from a plain program's by a relative error of at most 0.002.
Values may be sent and summed in bfloat16 or wider, within the bound.
A program may use at most 64 MiB of HBM per device.

v0:
```python
import jax
import jax.numpy as jnp
from jax import lax
from jax.sharding import PartitionSpec as P


def from_root(block, axis, owner):
    block = jnp.where(lax.axis_index(axis) == owner, block, jnp.zeros_like(block))
    return lax.psum(block, axis)


def from_behind(value, axis, steps):
    count = lax.axis_size(axis)
    first, last = (max(0, -steps), min(count, count - steps))
    return lax.ppermute(value, axis, [(source, source + steps) for source in range(first, last)])


def place_rows(placing, products):
    high_part = lax.optimization_barrier(products.astype(jnp.bfloat16))
    low_part = (products - high_part.astype(jnp.float32)).astype(jnp.bfloat16)
    first = jnp.einsum("bk,kie->bie", placing, high_part, preferred_element_type=jnp.float32)
    second = jnp.einsum("bk,kie->bie", placing, low_part, preferred_element_type=jnp.float32)
    return first + second


def per_device(
    excitation, pending, inverse, interaction, slot_row, slot_owner, slot_pos, needed, block_count
):
    row_blocks, block_size, _ = inverse.shape
    slot_total = interaction.shape[0]
    exc_width = excitation.shape[2]
    capacity = needed.shape[2]
    live_slots = jnp.arange(slot_total, dtype=jnp.int32) < block_count[0, 0]
    placing = (
        (slot_row[None, :] == jnp.arange(row_blocks, dtype=jnp.int32)[:, None])
        & live_slots[None, :]
    ).astype(jnp.bfloat16)
    need_table = needed[0]
    asked = lax.all_to_all(need_table, "rows", split_axis=0, concat_axis=0, tiled=True)
    send_index = asked.reshape(-1)
    source = slot_owner * capacity + slot_pos
    accumulated = pending[0]
    outputs = []
    for step_index in range(excitation.shape[0]):
        right_side = (excitation[step_index].astype(jnp.float32) - accumulated).reshape(
            row_blocks, block_size, exc_width
        )
        solved = jnp.einsum(
            "bij,bje->bie", inverse, right_side, precision=lax.Precision.HIGHEST
        ).astype(jnp.bfloat16)
        solved = from_root(solved, "lag", 0)
        outputs.append(solved.reshape(row_blocks * block_size, exc_width))
        outgoing = jnp.take(solved, send_index, axis=0)
        arrived = lax.all_to_all(outgoing, "rows", split_axis=0, concat_axis=0, tiled=True)
        picked = jnp.take(arrived, source, axis=0)
        products = jnp.einsum(
            "kij,kje->kie", interaction, picked, preferred_element_type=jnp.float32
        )
        lag_term = place_rows(placing, products)
        handed = from_behind(accumulated, "lag", -1)
        accumulated = handed + lag_term.reshape(row_blocks * block_size, exc_width)
    return (jnp.stack(outputs), accumulated[None])


def solution(mesh):
    in_specs = (
        P(None, "rows", None),
        P("lag", "rows", None),
        P("rows", None, None),
        P(("rows", "lag"), None, None),
        P(("rows", "lag")),
        P(("rows", "lag")),
        P(("rows", "lag")),
        P(("rows", "lag"), None, None),
        P("rows", "lag"),
    )
    out_specs = (P(None, "rows", None), P("lag", "rows", None))
    return jax.shard_map(
        per_device, mesh=mesh, in_specs=in_specs, out_specs=out_specs, check_vma=False
    )
```

profile of v0, /device:TPU:7, one launch (start us, length us, event | category | flops | bytes accessed | tf_op | source)
XLA Modules:
  0.0 424.5 jit_solution(6430174055130617571)
XLA Ops:
  8.7 4.6 %all-to-all-start = ((s32[4,1,2]{2,1,0:T(1,128)}), s32[4,1,2]{2,1,0:T(1,128)S(1)}, u32[]{:S(2)}, u32[]{:S(2)}) async-start(s32[4,1,2]{2,1,0:T(1,128)} %copy.47), calls=%async_computation | async-start | bytes 4096 | tf_op jit(solution)/shard_map/all_to_all | solution.py:39
  16.5 3.6 collective-permute-start
  22.8 47.3 %all-reduce.5.cloned.1.call-done = bf16[4,128,128]{1,2,0:T(8,128)(2,1)} async-done(((bf16[4,128,128]{1,2,0:T(8,128)(2,1)}), bf16[4,128,128]{1,2,0:T(8,128)(2,1)}) %all-reduce.5.cloned.1.call-update) | async-done | bytes 131088 | tf_op jit(solution)/shard_map/psum | solution.py:9
  72.3 4.3 %all-to-all-start.1 = ((bf16[8,128,128]{1,2,0:T(8,128)(2,1)}), bf16[8,128,128]{1,2,0:T(8,128)(2,1)S(1)}, u32[]{:S(2)}, u32[]{:S(2)}) async-start(bf16[8,128,128]{1,2,0:T(8,128)(2,1)} %broadcast_select_fusion.3), calls=%async_computation.1 | async-start | bytes 524288 | tf_op jit(solution)/shard_map/all_to_all | solution.py:54
  77.3 5.0 %all-to-all-done.1 = bf16[8,128,128]{1,2,0:T(8,128)(2,1)S(1)} async-done(((bf16[8,128,128]{1,2,0:T(8,128)(2,1)}), bf16[8,128,128]{1,2,0:T(8,128)(2,1)S(1)}, u32[]{:S(2)}, u32[]{:S(2)}) %all-to-all-start.1) | async-done | bytes 262176 | tf_op jit(solution)/shard_map/all_to_all | solution.py:54
  82.4 2.8 gather_fusion.1
  85.1 7.8 %bitcast_convert_fusion.3 = (bf16[96,128,128]{1,2,0:T(8,128)(2,1)}, f32[96,128,128]{2,1,0:T(8,128)}) fusion(bf16[96,128,128]{2,1,0:T(8,128)(2,1)S(1)} %copy-done, bf16[96,128,128]{1,2,0:T(8,128)(2,1)} %gather_fusion.1, pred[96]{0:T(512)(128)(4,1)S(1)} %get-tuple-element.10), kind=kOutput, calls=%fused_computation.18 | convolution fusion | flops 405798912 | bytes 15728736 | tf_op jit(solution)/shard_map/kij,kje->kie/dot_general | solution.py:56
  92.9 5.0 %copy.48 = bf16[96,128,128]{2,0,1:T(8,128)(2,1)} copy(bf16[96,128,128]{1,2,0:T(8,128)(2,1)} %get-tuple-element.12) | data formatting | bytes 6291456 | tf_op jit(solution)/shard_map/optimization_barrier | solution.py:19
  97.9 6.7 %fusion.3 = bf16[96,128,128]{1,2,0:T(8,128)(2,1)} fusion(f32[96,128,128]{2,1,0:T(8,128)} %get-tuple-element.13, bf16[96,128,128]{1,2,0:T(8,128)(2,1)} %get-tuple-element.12), kind=kLoop, calls=%fused_computation.19 | loop fusion | flops 4718592 | bytes 12582912 | tf_op jit(solution)/shard_map/convert_element_type | solution.py:20
  104.6 4.9 %copy.49 = bf16[96,128,128]{2,0,1:T(8,128)(2,1)} copy(bf16[96,128,128]{1,2,0:T(8,128)(2,1)} %fusion.3) | data formatting | bytes 6291456 | tf_op jit(solution)/shard_map/convert_element_type | solution.py:20
  116.0 53.3 %all-reduce.7.cloned.1.call-done = bf16[4,128,128]{1,2,0:T(8,128)(2,1)} async-done(((bf16[4,128,128]{1,2,0:T(8,128)(2,1)}), bf16[4,128,128]{1,2,0:T(8,128)(2,1)}) %all-reduce.7.cloned.1.call-update) | async-done | bytes 131088 | tf_op jit(solution)/shard_map/psum | solution.py:9
  171.6 4.3 %all-to-all-start.2 = ((bf16[8,128,128]{1,2,0:T(8,128)(2,1)}), bf16[8,128,128]{1,2,0:T(8,128)(2,1)S(1)}, u32[]{:S(2)}, u32[]{:S(2)}) async-start(bf16[8,128,128]{1,2,0:T(8,128)(2,1)} %broadcast_select_fusion.2), calls=%async_computation.2 | async-start | bytes 524288 | tf_op jit(solution)/shard_map/all_to_all | solution.py:54
  175.9 4.3 %collective-permute-start.1 = (f32[512,128]{1,0:T(8,128)}, f32[512,128]{1,0:T(8,128)}, u32[]{:S(2)}, u32[]{:S(2)}) collective-permute-start(f32[512,128]{1,0:T(8,128)} %get-tuple-element.9), channel_id=1, source_target_pairs={{1,0},{2,1},{3,2},{4,3},{5,4},{6,5},{7,6},{9,8},{10,9},{11,10},{12... | collective-permute-start | bytes 786440 | tf_op jit(solution)/shard_map/ppermute | solution.py:15
  184.3 7.9 %bitcast_convert_fusion.2 = (bf16[96,128,128]{1,2,0:T(8,128)(2,1)}, f32[96,128,128]{2,1,0:T(8,128)}) fusion(bf16[96,128,128]{2,1,0:T(8,128)(2,1)S(1)} %copy-done, bf16[96,128,128]{1,2,0:T(8,128)(2,1)} %gather_fusion.3, pred[96]{0:T(512)(128)(4,1)S(1)} %get-tuple-element.10), kind=kOutput, calls=%fused_computation.15 | convolution fusion | flops 405798912 | bytes 15728736 | tf_op jit(solution)/shard_map/kij,kje->kie/dot_general | solution.py:56
  192.2 4.9 %copy.53 = bf16[96,128,128]{2,0,1:T(8,128)(2,1)} copy(bf16[96,128,128]{1,2,0:T(8,128)(2,1)} %get-tuple-element.14) | data formatting | bytes 6291456 | tf_op jit(solution)/shard_map/optimization_barrier | solution.py:19
  197.1 6.9 %fusion.2 = bf16[96,128,128]{1,2,0:T(8,128)(2,1)} fusion(f32[96,128,128]{2,1,0:T(8,128)} %get-tuple-element.15, bf16[96,128,128]{1,2,0:T(8,128)(2,1)} %get-tuple-element.14), kind=kLoop, calls=%fused_computation.16 | loop fusion | flops 4718592 | bytes 12582912 | tf_op jit(solution)/shard_map/convert_element_type | solution.py:20
  204.5 4.9 %copy.54 = bf16[96,128,128]{2,0,1:T(8,128)(2,1)} copy(bf16[96,128,128]{1,2,0:T(8,128)(2,1)} %fusion.2) | data formatting | bytes 6291456 | tf_op jit(solution)/shard_map/convert_element_type | solution.py:20
  215.0 53.3 %all-reduce.9.cloned.1.call-done = bf16[4,128,128]{1,2,0:T(8,128)(2,1)} async-done(((bf16[4,128,128]{1,2,0:T(8,128)(2,1)}), bf16[4,128,128]{1,2,0:T(8,128)(2,1)}) %all-reduce.9.cloned.1.call-update) | async-done | bytes 131088 | tf_op jit(solution)/shard_map/psum | solution.py:9
  270.6 4.3 %all-to-all-start.3 = ((bf16[8,128,128]{1,2,0:T(8,128)(2,1)}), bf16[8,128,128]{1,2,0:T(8,128)(2,1)S(1)}, u32[]{:S(2)}, u32[]{:S(2)}) async-start(bf16[8,128,128]{1,2,0:T(8,128)(2,1)} %broadcast_select_fusion.1), calls=%async_computation.3 | async-start | bytes 524288 | tf_op jit(solution)/shard_map/all_to_all | solution.py:54
  274.9 4.3 %collective-permute-start.2 = (f32[512,128]{1,0:T(8,128)}, f32[512,128]{1,0:T(8,128)}, u32[]{:S(2)}, u32[]{:S(2)}) collective-permute-start(f32[512,128]{1,0:T(8,128)} %get-tuple-element.7), channel_id=1, source_target_pairs={{1,0},{2,1},{3,2},{4,3},{5,4},{6,5},{7,6},{9,8},{10,9},{11,10},{12... | collective-permute-start | bytes 786440 | tf_op jit(solution)/shard_map/ppermute | solution.py:15
  283.4 7.9 %bitcast_convert_fusion.1 = (bf16[96,128,128]{1,2,0:T(8,128)(2,1)}, f32[96,128,128]{2,1,0:T(8,128)}) fusion(bf16[96,128,128]{2,1,0:T(8,128)(2,1)S(1)} %copy-done, bf16[96,128,128]{1,2,0:T(8,128)(2,1)} %gather_fusion.5, pred[96]{0:T(512)(128)(4,1)S(1)} %get-tuple-element.10), kind=kOutput, calls=%fused_computation.12 | convolution fusion | flops 405798912 | bytes 15728736 | tf_op jit(solution)/shard_map/kij,kje->kie/dot_general | solution.py:56
  291.3 4.9 %copy.58 = bf16[96,128,128]{2,0,1:T(8,128)(2,1)} copy(bf16[96,128,128]{1,2,0:T(8,128)(2,1)} %get-tuple-element.16) | data formatting | bytes 6291456 | tf_op jit(solution)/shard_map/optimization_barrier | solution.py:19
  296.2 6.9 %fusion.1 = bf16[96,128,128]{1,2,0:T(8,128)(2,1)} fusion(f32[96,128,128]{2,1,0:T(8,128)} %get-tuple-element.17, bf16[96,128,128]{1,2,0:T(8,128)(2,1)} %get-tuple-element.16), kind=kLoop, calls=%fused_computation.13 | loop fusion | flops 4718592 | bytes 12582912 | tf_op jit(solution)/shard_map/convert_element_type | solution.py:20
  303.6 4.9 %copy.59 = bf16[96,128,128]{2,0,1:T(8,128)(2,1)} copy(bf16[96,128,128]{1,2,0:T(8,128)(2,1)} %fusion.1) | data formatting | bytes 6291456 | tf_op jit(solution)/shard_map/convert_element_type | solution.py:20
  314.1 53.3 %all-reduce.11.cloned.1.call-done = bf16[4,128,128]{1,2,0:T(8,128)(2,1)} async-done(((bf16[4,128,128]{1,2,0:T(8,128)(2,1)}), bf16[4,128,128]{1,2,0:T(8,128)(2,1)}) %all-reduce.11.cloned.1.call-update) | async-done | bytes 131088 | tf_op jit(solution)/shard_map/psum | solution.py:9
  370.3 4.3 %all-to-all-start.4 = ((bf16[8,128,128]{1,2,0:T(8,128)(2,1)}), bf16[8,128,128]{1,2,0:T(8,128)(2,1)S(1)}, u32[]{:S(2)}, u32[]{:S(2)}) async-start(bf16[8,128,128]{1,2,0:T(8,128)(2,1)} %broadcast_select_fusion), calls=%async_computation.4 | async-start | bytes 524288 | tf_op jit(solution)/shard_map/all_to_all | solution.py:54
  378.1 4.3 %collective-permute-start.3 = (f32[512,128]{1,0:T(8,128)}, f32[512,128]{1,0:T(8,128)}, u32[]{:S(2)}, u32[]{:S(2)}) collective-permute-start(f32[512,128]{1,0:T(8,128)} %get-tuple-element.5), channel_id=1, source_target_pairs={{1,0},{2,1},{3,2},{4,3},{5,4},{6,5},{7,6},{9,8},{10,9},{11,10},{12... | collective-permute-start | bytes 786440 | tf_op jit(solution)/shard_map/ppermute | solution.py:15
  386.0 2.7 gather_fusion.7
  388.7 7.9 %bitcast_convert_fusion = (bf16[96,128,128]{1,2,0:T(8,128)(2,1)}, f32[96,128,128]{2,1,0:T(8,128)}) fusion(bf16[96,128,128]{2,1,0:T(8,128)(2,1)S(1)} %copy-done, bf16[96,128,128]{1,2,0:T(8,128)(2,1)} %gather_fusion.7, pred[96]{0:T(512)(128)(4,1)S(1)} %get-tuple-element.10), kind=kOutput, calls=%fused_computation.9 | convolution fusion | flops 405798912 | bytes 15728736 | tf_op jit(solution)/shard_map/kij,kje->kie/dot_general | solution.py:56
  396.6 4.9 %copy.63 = bf16[96,128,128]{2,0,1:T(8,128)(2,1)} copy(bf16[96,128,128]{1,2,0:T(8,128)(2,1)} %get-tuple-element.18) | data formatting | bytes 6291456 | tf_op jit(solution)/shard_map/optimization_barrier | solution.py:19
  401.5 6.9 %fusion = bf16[96,128,128]{1,2,0:T(8,128)(2,1)} fusion(f32[96,128,128]{2,1,0:T(8,128)} %get-tuple-element.19, bf16[96,128,128]{1,2,0:T(8,128)(2,1)} %get-tuple-element.18), kind=kLoop, calls=%fused_computation.10 | loop fusion | flops 4718592 | bytes 12582912 | tf_op jit(solution)/shard_map/convert_element_type | solution.py:20
  408.9 4.9 %copy.64 = bf16[96,128,128]{2,0,1:T(8,128)(2,1)} copy(bf16[96,128,128]{1,2,0:T(8,128)(2,1)} %fusion) | data formatting | bytes 6291456 | tf_op jit(solution)/shard_map/convert_element_type | solution.py:20
  (83 shorter events, 55.6 us)
Async XLA Ops:
  7.2 78.0 %copy-start = (bf16[96,128,128]{2,1,0:T(8,128)(2,1)S(1)}, bf16[96,128,128]{2,1,0:T(8,128)(2,1)}, u32[]{:S(2)}) copy-start(bf16[96,128,128]{2,1,0:T(8,128)(2,1)} %param.16) | copy-start | bytes 9437188
  8.7 12.8 %all-to-all-start = ((s32[4,1,2]{2,1,0:T(1,128)}), s32[4,1,2]{2,1,0:T(1,128)S(1)}, u32[]{:S(2)}, u32[]{:S(2)}) async-start(s32[4,1,2]{2,1,0:T(1,128)} %copy.47), calls=%async_computation | async-start | bytes 4096 | tf_op jit(solution)/shard_map/all_to_all | solution.py:39
  13.3 56.8 %all-reduce.5.cloned.1.call-start = ((), (), s32[]{:S(2)}) async-start(), calls=%async_computation.5 | async-start | bytes 262144 | tf_op jit(solution)/shard_map/psum | solution.py:9
  16.5 96.4 %collective-permute-start = (f32[512,128]{1,0:T(8,128)}, f32[512,128]{1,0:T(8,128)}, u32[]{:S(2)}, u32[]{:S(2)}) collective-permute-start(f32[512,128]{1,0:T(8,128)} %bitcast.100), channel_id=1, source_target_pairs={{1,0},{2,1},{3,2},{4,3},{5,4},{6,5},{7,6},{9,8},{10,9},{11,10},{12... | collective-permute-start | bytes 786440 | tf_op jit(solution)/shard_map/ppermute | solution.py:15
  22.7 247.1 %copy-start.9 = (pred[8]{0:T(512)(128)(4,1)}, pred[8]{0:T(512)(128)(4,1)S(1)}, u32[]{:S(2)}) copy-start(pred[8]{0:T(512)(128)(4,1)S(1)} %compare_and_fusion.1) | copy-start | bytes 28
  72.3 10.0 %all-to-all-start.1 = ((bf16[8,128,128]{1,2,0:T(8,128)(2,1)}), bf16[8,128,128]{1,2,0:T(8,128)(2,1)S(1)}, u32[]{:S(2)}, u32[]{:S(2)}) async-start(bf16[8,128,128]{1,2,0:T(8,128)(2,1)} %broadcast_select_fusion.3), calls=%async_computation.1 | async-start | bytes 524288 | tf_op jit(solution)/shard_map/all_to_all | solution.py:54
  76.6 92.6 %all-reduce.7.cloned.1.call-start = ((), (), s32[]{:S(2)}) async-start(), calls=%async_computation.6 | async-start | bytes 262144 | tf_op jit(solution)/shard_map/psum | solution.py:9
  109.5 2.8 copy-start.4
  112.4 2.3 copy-start.5
  171.6 10.0 %all-to-all-start.2 = ((bf16[8,128,128]{1,2,0:T(8,128)(2,1)}), bf16[8,128,128]{1,2,0:T(8,128)(2,1)S(1)}, u32[]{:S(2)}, u32[]{:S(2)}) async-start(bf16[8,128,128]{1,2,0:T(8,128)(2,1)} %broadcast_select_fusion.2), calls=%async_computation.2 | async-start | bytes 524288 | tf_op jit(solution)/shard_map/all_to_all | solution.py:54
  175.9 92.4 %all-reduce.9.cloned.1.call-start = ((), (), s32[]{:S(2)}) async-start(), calls=%async_computation.7 | async-start | bytes 262144 | tf_op jit(solution)/shard_map/psum | solution.py:9
  175.9 36.1 %collective-permute-start.1 = (f32[512,128]{1,0:T(8,128)}, f32[512,128]{1,0:T(8,128)}, u32[]{:S(2)}, u32[]{:S(2)}) collective-permute-start(f32[512,128]{1,0:T(8,128)} %get-tuple-element.9), channel_id=1, source_target_pairs={{1,0},{2,1},{3,2},{4,3},{5,4},{6,5},{7,6},{9,8},{10,9},{11,10},{12... | collective-permute-start | bytes 786440 | tf_op jit(solution)/shard_map/ppermute | solution.py:15
  197.1 6.9 %copy-start.1 = (bf16[96,128,128]{2,0,1:T(8,128)(2,1)S(1)}, bf16[96,128,128]{2,0,1:T(8,128)(2,1)}, u32[]{:S(2)}) copy-start(bf16[96,128,128]{2,0,1:T(8,128)(2,1)} %copy.53) | copy-start | bytes 9437188
  209.5 4.3 %copy-start.6 = (f32[4,128,128]{2,1,0:T(8,128)S(1)}, f32[4,128,128]{2,1,0:T(8,128)}, u32[]{:S(2)}) copy-start(f32[4,128,128]{2,1,0:T(8,128)} %param.15) | copy-start | bytes 786436
  270.6 10.0 %all-to-all-start.3 = ((bf16[8,128,128]{1,2,0:T(8,128)(2,1)}), bf16[8,128,128]{1,2,0:T(8,128)(2,1)S(1)}, u32[]{:S(2)}, u32[]{:S(2)}) async-start(bf16[8,128,128]{1,2,0:T(8,128)(2,1)} %broadcast_select_fusion.1), calls=%async_computation.3 | async-start | bytes 524288 | tf_op jit(solution)/shard_map/all_to_all | solution.py:54
  274.9 92.4 %all-reduce.11.cloned.1.call-start = ((), (), s32[]{:S(2)}) async-start(), calls=%async_computation.8 | async-start | bytes 262144 | tf_op jit(solution)/shard_map/psum | solution.py:9
  274.9 36.1 %collective-permute-start.2 = (f32[512,128]{1,0:T(8,128)}, f32[512,128]{1,0:T(8,128)}, u32[]{:S(2)}, u32[]{:S(2)}) collective-permute-start(f32[512,128]{1,0:T(8,128)} %get-tuple-element.7), channel_id=1, source_target_pairs={{1,0},{2,1},{3,2},{4,3},{5,4},{6,5},{7,6},{9,8},{10,9},{11,10},{12... | collective-permute-start | bytes 786440 | tf_op jit(solution)/shard_map/ppermute | solution.py:15
  296.2 6.9 %copy-start.2 = (bf16[96,128,128]{2,0,1:T(8,128)(2,1)S(1)}, bf16[96,128,128]{2,0,1:T(8,128)(2,1)}, u32[]{:S(2)}) copy-start(bf16[96,128,128]{2,0,1:T(8,128)(2,1)} %copy.58) | copy-start | bytes 9437188
  308.5 4.3 %copy-start.7 = (f32[4,128,128]{2,1,0:T(8,128)S(1)}, f32[4,128,128]{2,1,0:T(8,128)}, u32[]{:S(2)}) copy-start(f32[4,128,128]{2,1,0:T(8,128)} %param.15) | copy-start | bytes 786436
  308.5 66.1 %copy-start.8 = (bf16[4,128,128]{1,2,0:T(8,128)(2,1)S(1)}, bf16[4,128,128]{1,2,0:T(8,128)(2,1)}, u32[]{:S(2)}) copy-start(bf16[4,128,128]{1,2,0:T(8,128)(2,1)} %all-reduce.5.cloned.1.call-done) | copy-start | bytes 393220
  370.3 15.7 %all-to-all-start.4 = ((bf16[8,128,128]{1,2,0:T(8,128)(2,1)}), bf16[8,128,128]{1,2,0:T(8,128)(2,1)S(1)}, u32[]{:S(2)}, u32[]{:S(2)}) async-start(bf16[8,128,128]{1,2,0:T(8,128)(2,1)} %broadcast_select_fusion), calls=%async_computation.4 | async-start | bytes 524288 | tf_op jit(solution)/shard_map/all_to_all | solution.py:54
  378.1 38.2 %collective-permute-start.3 = (f32[512,128]{1,0:T(8,128)}, f32[512,128]{1,0:T(8,128)}, u32[]{:S(2)}, u32[]{:S(2)}) collective-permute-start(f32[512,128]{1,0:T(8,128)} %get-tuple-element.5), channel_id=1, source_target_pairs={{1,0},{2,1},{3,2},{4,3},{5,4},{6,5},{7,6},{9,8},{10,9},{11,10},{12... | collective-permute-start | bytes 786440 | tf_op jit(solution)/shard_map/ppermute | solution.py:15
  401.5 6.9 %copy-start.3 = (bf16[96,128,128]{2,0,1:T(8,128)(2,1)S(1)}, bf16[96,128,128]{2,0,1:T(8,128)(2,1)}, u32[]{:S(2)}) copy-start(bf16[96,128,128]{2,0,1:T(8,128)(2,1)} %copy.63) | copy-start | bytes 9437188
Sparse Core Ops, SparseCore 0:
  17.7 52.2 all-reduce.4
  116.1 53.0 all-reduce.6
  215.1 53.1 all-reduce.8
  314.2 53.0 all-reduce.10
where the time goes:
time: 428 us; the launch traced here: 425 us
  waiting for transfers between devices  215 us (50%)
  local copies, waits for them, and re-layouts  64 us (15%)
  matrix products  49.4 us (12%)
  other arithmetic  43.1 us (10%)
  starting transfers between devices  38.5 us (9%)
  between operations  14.6 us (3%)
    psum x4, waiting for transfers between devices, from_root(): return lax.psum(block, axis)  207 us
    dot_general x4, matrix products, per_device(): jnp.einsum('kij,kje->kie', interaction, picked, preferred_element_type=jn...  31.5 us
    convert_element_type x4, other arithmetic, place_rows(): low_part = (products - high_part.astype(jnp.float32)).astype(jnp.bfloat16)  27.3 us
    optimization_barrier x4, local copies, waits for them, and re-layouts, place_rows(): high_part = lax.optimization_barrier(products.astype(jnp.bfloat16))  19.8 us
    convert_element_type x4, local copies, waits for them, and re-layouts, place_rows(): low_part = (products - high_part.astype(jnp.float32)).astype(jnp.bfloat16)  19.7 us
    all_to_all x4, starting transfers between devices, per_device(): lax.all_to_all(outgoing, 'rows', split_axis=0, concat_axis=0, tiled=True)  17.3 us
    ppermute x4, starting transfers between devices, from_behind(): lax.ppermute(value, axis, [(source, source + steps) for source in range(f...  16.6 us
    gather x4, local copies, waits for them, and re-layouts, per_device(): picked = jnp.take(arrived, source, axis=0)  10.9 us
  transfers between devices with their start and end apart: 13, of which 7 were waited for; matrix products, arithmetic and copies ran while one was open for 32% of the time, Pallas kernels for 0%

commit v1 on v0

v1 whole, which is shorter than its diff:
```python
import functools

import jax
import jax.numpy as jnp
from jax import lax
from jax.experimental import pallas as pl
from jax.experimental.pallas import tpu as pltpu
from jax.sharding import PartitionSpec as P

MESH = pl.DeviceIdType.MESH


def collapse_kernel(chunk, row_ref, owner_ref, pos_ref, count_ref, block_ref, high_ref, low_ref, total):
    row_blocks, columns, block_size, _ = total.shape
    capacity = count_ref[1]
    first = pl.program_id(0) * chunk

    @pl.when(pl.program_id(0) == 0)
    def _():
        total[...] = jnp.zeros_like(total)

    def add_slot(index, carry):
        slot = first + index
        row = row_ref[slot]
        column = owner_ref[slot] * capacity + pos_ref[slot]
        total[row, column] += block_ref[index].astype(jnp.float32)
        return carry

    live = jnp.clip(count_ref[0] - first, 0, chunk)
    lax.fori_loop(0, live, add_slot, 0)

    @pl.when(pl.program_id(0) == pl.num_programs(0) - 1)
    def _():
        for row in range(row_blocks):
            for column in range(columns):
                value = total[row, column]
                high = value.astype(jnp.bfloat16)
                low = (value - high.astype(jnp.float32)).astype(jnp.bfloat16)
                place = (pl.ds(row * block_size, block_size), pl.ds(column * block_size, block_size))
                high_ref[place] = high
                low_ref[place] = low


def collapse(interaction, slot_row, slot_owner, slot_pos, block_count, row_blocks, columns, capacity):
    slots, block_size, _ = interaction.shape
    chunk = max(size for size in range(1, 17) if slots % size == 0)
    count = jnp.stack([block_count[0, 0], jnp.int32(capacity)])
    shape = (row_blocks * block_size, columns * block_size)
    whole = pl.BlockSpec(shape, lambda step, *_: (0, 0))
    return pl.pallas_call(
        functools.partial(collapse_kernel, chunk),
        grid_spec=pltpu.PrefetchScalarGridSpec(
            num_scalar_prefetch=4,
            grid=(slots // chunk,),
            in_specs=[pl.BlockSpec((chunk, block_size, block_size), lambda step, *_: (step, 0, 0))],
            out_specs=[whole, whole],
            scratch_shapes=[pltpu.VMEM((row_blocks, columns, block_size, block_size), jnp.float32)],
        ),
        out_shape=[jax.ShapeDtypeStruct(shape, jnp.bfloat16)] * 2,
        compiler_params=pltpu.CompilerParams(vmem_limit_bytes=40 * 1024 * 1024),
    )(slot_row, slot_owner, slot_pos, count, interaction)


def window_kernel(
    rows, lags, steps, row_blocks, capacity,
    excitation, pending, inverse, table, needed, high_hbm, low_hbm,
    currents, carried,
    high, low, own, sending, landed, handed, summed, asked, asked_scalar,
    row_send, row_recv, lag_send, lag_recv, hand_send, hand_recv, ask_send, ask_recv, local_sem, out_sem,
):
    row = lax.axis_index("rows")
    lag = lax.axis_index("lag")
    block_size = inverse.shape[1]

    barrier = pltpu.get_barrier_semaphore()
    for away in range(1, rows):
        pl.semaphore_signal(barrier, inc=1, device_id=(lax.rem(row + away, rows), lag), device_id_type=MESH)
    for away in range(1, lags):
        pl.semaphore_signal(barrier, inc=1, device_id=(row, lax.rem(lag + away, lags)), device_id_type=MESH)

    fetch_high = pltpu.make_async_copy(high_hbm, high, local_sem.at[0])
    fetch_low = pltpu.make_async_copy(low_hbm, low, local_sem.at[1])
    fetch_high.start()
    fetch_low.start()

    def solve(step):
        for block in range(row_blocks):
            place = pl.ds(block * block_size, block_size)
            before = pending[0, place] if step == 0 else summed[step - 1, place]
            right_side = excitation[step, place].astype(jnp.float32) - before
            solved = jnp.dot(
                inverse[block], right_side, precision=lax.Precision.HIGHEST,
                preferred_element_type=jnp.float32,
            )
            own[step][block] = solved.astype(jnp.bfloat16)

    @pl.when(lag == 0)
    def _():
        solve(0)

    pl.semaphore_wait(barrier, rows + lags - 2)

    def ask_copy(away):
        target = lax.rem(row + away, rows)
        return pltpu.make_async_remote_copy(
            src_ref=table, dst_ref=asked.at[away - 1], send_sem=ask_send.at[away - 1],
            recv_sem=ask_recv.at[away - 1], device_id=(target, lag), device_id_type=MESH,
        )

    def row_copy(step, away):
        target = lax.rem(row + away, rows)
        return pltpu.make_async_remote_copy(
            src_ref=sending.at[step, away - 1], dst_ref=landed.at[step, row],
            send_sem=row_send.at[step, away - 1], recv_sem=row_recv.at[step, away - 1],
            device_id=(target, lag), device_id_type=MESH,
        )

    def lag_copy(step, target, which):
        return pltpu.make_async_remote_copy(
            src_ref=own[step], dst_ref=own[step],
            send_sem=lag_send.at[step, which], recv_sem=lag_recv.at[step],
            device_id=(row, target), device_id_type=MESH,
        )

    def hand_copy(step):
        source = pending.at[0] if step == 0 else summed.at[step - 1]
        return pltpu.make_async_remote_copy(
            src_ref=source, dst_ref=handed.at[step],
            send_sem=hand_send.at[step], recv_sem=hand_recv.at[step],
            device_id=(row, lax.rem(lag + lags - 1, lags)), device_id_type=MESH,
        )

    def out_copy(step):
        return pltpu.make_async_copy(own[step], currents.at[step], out_sem.at[step])

    for away in range(1, rows):
        ask_copy(away).start()

    @pl.when(lag > 0)
    def _():
        hand_copy(0).start()

    to_scalar = pltpu.make_async_copy(asked, asked_scalar, local_sem.at[2])
    evens = list(range(2, lags, 2))
    forwards = (lag > 0) & (lax.rem(lag, 2) == 0) & (lag + 1 < lags)

    for step in range(steps):
        last = step == steps - 1

        @pl.when(lag == 0)
        def _():
            if step > 0:
                solve(step)

        @pl.when(lag > 0)
        def _():
            lag_copy(step, 0, 0).wait_recv()

        if step == 0:
            for away in range(1, rows):
                ask_copy(away).wait_recv()
            to_scalar.start()
            to_scalar.wait()

        @pl.when(forwards)
        def _():
            lag_copy(step, lag + 1, 0).start()

        if last:
            @pl.when(lag == 0)
            def _():
                lag_copy(step, 1, 0).start()
                for place, target in enumerate(evens):
                    lag_copy(step, target, place + 1).start()

        for away in range(1, rows):
            for entry in range(capacity):
                sending[step, away - 1, entry] = own[step][asked_scalar[rows - away - 1, row, entry]]
            row_copy(step, away).start()

        if not last:
            @pl.when(lag == 0)
            def _():
                for place, target in enumerate(evens):
                    lag_copy(step, target, place + 1).start()

        out_copy(step).start()
        for entry in range(capacity):
            landed[step, row, entry] = own[step][needed[row, entry]]

        for away in range(1, rows):
            row_copy(step, away).wait_recv()

        if not last:
            @pl.when(lag == 0)
            def _():
                lag_copy(step, 1, 0).start()

        if step == 0:
            fetch_high.wait()
            fetch_low.wait()

            @pl.when(lag == lags - 1)
            def _():
                handed[...] = jnp.zeros_like(handed)

        values = landed[step].reshape(rows * capacity * block_size, landed.shape[-1])
        product = jnp.dot(high[...], values, preferred_element_type=jnp.float32)
        product += jnp.dot(low[...], values, preferred_element_type=jnp.float32)

        @pl.when(lag < lags - 1)
        def _():
            hand_copy(step).wait_recv()

        summed[step] = handed[step] + product
        if not last:
            @pl.when(lag > 0)
            def _():
                hand_copy(step + 1).start()

    finish = pltpu.make_async_copy(summed.at[steps - 1], carried.at[0], local_sem.at[3])
    finish.start()

    for away in range(1, rows):
        ask_copy(away).wait_send()
    for step in range(steps):
        for away in range(1, rows):
            row_copy(step, away).wait_send()
        out_copy(step).wait()

        @pl.when(lag > 0)
        def _():
            hand_copy(step).wait_send()

        @pl.when(forwards)
        def _():
            lag_copy(step, lag + 1, 0).wait_send()

        @pl.when(lag == 0)
        def _():
            lag_copy(step, 1, 0).wait_send()
            for place, target in enumerate(evens):
                lag_copy(step, target, place + 1).wait_send()

    finish.wait()


def per_device(
    excitation, pending, inverse, interaction, slot_row, slot_owner, slot_pos, needed, block_count
):
    row_blocks, block_size, _ = inverse.shape
    steps, unknowns, width = excitation.shape
    rows, capacity = needed.shape[1:]
    lags = lax.axis_size("lag")
    columns = rows * capacity
    high, low = collapse(
        interaction, slot_row, slot_owner, slot_pos, block_count, row_blocks, columns, capacity
    )
    table = jnp.pad(needed[0], ((0, -rows % 8), (0, -capacity % 128)))
    vmem = pl.BlockSpec(memory_space=pltpu.VMEM)
    smem = pl.BlockSpec(memory_space=pltpu.SMEM)
    hbm = pl.BlockSpec(memory_space=pl.ANY)
    dma = pltpu.SemaphoreType.DMA
    evens = len(range(2, lags, 2))
    return pl.pallas_call(
        functools.partial(window_kernel, rows, lags, steps, row_blocks, capacity),
        out_shape=[
            jax.ShapeDtypeStruct((steps, row_blocks, block_size, width), jnp.bfloat16),
            jax.ShapeDtypeStruct((1, unknowns, width), jnp.float32),
        ],
        in_specs=[vmem, vmem, vmem, vmem, smem, hbm, hbm],
        out_specs=[hbm, hbm],
        scratch_shapes=[
            pltpu.VMEM(high.shape, jnp.bfloat16),
            pltpu.VMEM(low.shape, jnp.bfloat16),
            [pltpu.VMEM((row_blocks, block_size, width), jnp.bfloat16)] * steps,
            pltpu.VMEM((steps, rows - 1, capacity, block_size, width), jnp.bfloat16),
            pltpu.VMEM((steps, rows, capacity, block_size, width), jnp.bfloat16),
            pltpu.VMEM((steps, unknowns, width), jnp.float32),
            pltpu.VMEM((steps, unknowns, width), jnp.float32),
            pltpu.VMEM((rows - 1,) + table.shape, jnp.int32),
            pltpu.SMEM((rows - 1,) + table.shape, jnp.int32),
            dma((steps, rows - 1)),
            dma((steps, rows - 1)),
            dma((steps, evens + 1)),
            dma((steps,)),
            dma((steps,)),
            dma((steps,)),
            dma((rows - 1,)),
            dma((rows - 1,)),
            dma((4,)),
            dma((steps,)),
        ],
        compiler_params=pltpu.CompilerParams(
            collective_id=0, has_side_effects=True, vmem_limit_bytes=48 * 1024 * 1024
        ),
    )(excitation, pending, inverse, table, needed[0], high, low)


def solution(mesh):
    in_specs = (
        P(None, "rows", None),
        P("lag", "rows", None),
        P("rows", None, None),
        P(("rows", "lag"), None, None),
        P(("rows", "lag")),
        P(("rows", "lag")),
        P(("rows", "lag")),
        P(("rows", "lag"), None, None),
        P("rows", "lag"),
    )
    out_specs = (P(None, "rows", None), P("lag", "rows", None))

    def body(*arrays):
        currents, carried = per_device(*arrays)
        return currents.reshape(arrays[0].shape), carried

    return jax.shard_map(body, mesh=mesh, in_specs=in_specs, out_specs=out_specs, check_vma=False)
```

time: 428 us -> 56 us (0.13)
  waiting for transfers between devices: 215 us -> 0 us
  local copies, waits for them, and re-layouts: 64 us -> 6.13 us
  matrix products: 49.4 us -> 0 us
  Pallas kernels: 0 us -> 47.7 us
  other arithmetic: 43.1 us -> 0.08 us
  starting transfers between devices: 38.5 us -> 0 us
  between operations: 14.6 us -> 1.32 us
    psum x4 -> x0, waiting for transfers between devices: 207 us -> none  [from_root(): return lax.psum(block, axis)]
    dot_general x16 -> x0, matrix products: 49.4 us -> none  [the longest x4 31.5 us: per_device(): jnp.einsum('kij,kje->kie', interaction, picked, preferred_element_type=jn...]
    pallas_call x0 -> x2, Pallas kernels: none -> 47.7 us  [the longest x1 46 us: per_device(): pl.pallas_call(functools.partial(window_kernel, rows, lags, steps, row_bl...]
    convert_element_type x4 -> x0, other arithmetic: 27.3 us -> none  [place_rows(): low_part = (products - high_part.astype(jnp.float32)).astype(jnp.bfloat16)]
    all_to_all x5 -> x0, starting transfers between devices: 21.9 us -> none  [the longest x4 17.3 us: per_device(): lax.all_to_all(outgoing, 'rows', split_axis=0, concat_axis=0, tiled=True)]
    optimization_barrier x4 -> x0, local copies, waits for them, and re-layouts: 19.8 us -> none  [place_rows(): high_part = lax.optimization_barrier(products.astype(jnp.bfloat16))]
    convert_element_type x4 -> x0, local copies, waits for them, and re-layouts: 19.7 us -> none  [place_rows(): low_part = (products - high_part.astype(jnp.float32)).astype(jnp.bfloat16)]
    gather x8 -> x0, local copies, waits for them, and re-layouts: 16.9 us -> none  [the longest x4 10.9 us: per_device(): picked = jnp.take(arrived, source, axis=0)]
  transfers between devices with their start and end apart: 13 -> 0, of which waited for: 7 -> 0; matrix products, arithmetic and copies ran while one was open for 32% -> 0% of each run, Pallas kernels for 0% -> 0%
where the time goes in v1:
time: 56 us; the launch traced here: 55.2 us
  Pallas kernels  47.7 us (85%)
  local copies, waits for them, and re-layouts  6.13 us (11%)
  between operations  1.32 us (2%)
    pallas_call x1, Pallas kernels, per_device(): pl.pallas_call(functools.partial(window_kernel, rows, lags, steps, row_bl...  46 us
    unnamed x16, local copies, waits for them, and re-layouts  5.36 us
    pallas_call x1, Pallas kernels, collapse(): pl.pallas_call(functools.partial(collapse_kernel, chunk), grid_spec=pltpu...  1.77 us

profile of v1, /device:TPU:7, one launch (start us, length us, event | category | flops | bytes accessed | tf_op | source)
XLA Modules:
  0.0 55.2 jit_solution(6341471671601745054)
XLA Ops:
  1.3 0.1 pad_add_fusion.count_ref
  1.4 0.8 %copy.11.needed = s32[4,2]{1,0:T(4,128)S(1)} copy(s32[4,2]{0,1:T(2,128)} %bitcast.5) | data formatting | bytes 64 | tf_op jit(solution)/shard_map/squeeze | solution.py:259
  2.1 0.0 copy-start
  2.1 1.9 %copy-done = bf16[96,128,128]{2,1,0:T(8,128)(2,1)S(1)} copy-done((bf16[96,128,128]{2,1,0:T(8,128)(2,1)S(1)}, bf16[96,128,128]{2,1,0:T(8,128)(2,1)}, u32[]{:S(2)}) %copy-start) | copy-done | bytes 3145752
  4.0 0.0 copy-start.4
  4.0 0.7 %copy-done.4 = s32[96]{0:T(128)S(1)} copy-done((s32[96]{0:T(128)S(1)}, s32[96]{0:T(128)}, u32[]{:S(2)}) %copy-start.4) | copy-done | bytes 408
  4.7 0.0 copy-start.5
  4.7 0.7 %copy-done.5 = s32[96]{0:T(128)S(1)} copy-done((s32[96]{0:T(128)S(1)}, s32[96]{0:T(128)}, u32[]{:S(2)}) %copy-start.5) | copy-done | bytes 408
  5.3 0.0 copy-start.6
  5.3 0.7 %copy-done.6 = s32[96]{0:T(128)S(1)} copy-done((s32[96]{0:T(128)S(1)}, s32[96]{0:T(128)}, u32[]{:S(2)}) %copy-start.6) | copy-done | bytes 408
  6.0 0.0 copy-start.1
  6.0 0.0 copy-start.2
  6.0 0.0 copy-start.3
  6.0 1.8 %shard_map.104 = (bf16[512,1024]{1,0:T(8,128)(2,1)S(1)}, bf16[512,1024]{1,0:T(8,128)(2,1)S(1)}) custom-call(s32[96]{0:T(128)S(1)} %copy-done.4, s32[96]{0:T(128)S(1)} %copy-done.5, s32[96]{0:T(128)S(1)} %copy-done.6, s32[2]{0:T(128)S(1)} %pad_add_fusion.count_ref, bf16[96,128,128]{2,1,0:T(8,128)(2,1)S(1)} %copy-done), custom_call_target="tpu_custom_call" | custom-call | tf_op jit(solution)/shard_map/pallas_call | solution.py:50
  7.8 0.0 copy-done.1
  7.8 0.0 copy-done.2
  7.8 0.0 copy-done.3
  7.8 46.0 %shard_map.105 = (bf16[4,4,128,128]{3,2,1,0:T(8,128)(2,1)S(1)}, f32[1,512,128]{2,1,0:T(8,128)S(1)}) custom-call(bf16[4,512,128]{2,1,0:T(8,128)(2,1)S(1)} %copy-done.1, f32[1,512,128]{2,1,0:T(8,128)S(1)} %copy-done.2, f32[4,128,128]{2,1,0:T(8,128)S(1)} %copy-done.3, s32[8,128]{1,0:T(8,128)S(1)} %pad.4.table, s32[4,2]{1,0:T(4,128)S(1)} %copy.11.needed, ...), custom_call_target="tpu_custom_call" | custom-call | tf_op jit(solution)/shard_map/pallas_call | solution.py:265
  53.8 0.8 %copy.16 = bf16[4,512,128]{2,1,0:T(8,128)(2,1)} copy(bf16[4,512,128]{2,1,0:T(8,128)(2,1)S(1)} %bitcast.4) | data formatting | bytes 1048576
  54.5 0.7 %copy.17 = f32[1,512,128]{2,1,0:T(8,128)} copy(f32[1,512,128]{2,1,0:T(8,128)S(1)} %get-tuple-element.13) | data formatting | bytes 524288
  (1 shorter events, 0.0 us)
Async XLA Ops:
  2.1 1.9 %copy-start = (bf16[96,128,128]{2,1,0:T(8,128)(2,1)S(1)}, bf16[96,128,128]{2,1,0:T(8,128)(2,1)}, u32[]{:S(2)}) copy-start(bf16[96,128,128]{2,1,0:T(8,128)(2,1)} %block_ref.1) | copy-start | bytes 9437188
  4.0 0.7 %copy-start.4 = (s32[96]{0:T(128)S(1)}, s32[96]{0:T(128)}, u32[]{:S(2)}) copy-start(s32[96]{0:T(128)} %row_ref.1) | copy-start | bytes 1156
  4.7 0.7 %copy-start.5 = (s32[96]{0:T(128)S(1)}, s32[96]{0:T(128)}, u32[]{:S(2)}) copy-start(s32[96]{0:T(128)} %owner_ref.1) | copy-start | bytes 1156
  5.3 0.7 %copy-start.6 = (s32[96]{0:T(128)S(1)}, s32[96]{0:T(128)}, u32[]{:S(2)}) copy-start(s32[96]{0:T(128)} %pos_ref.1) | copy-start | bytes 1156
  6.0 1.8 %copy-start.1 = (bf16[4,512,128]{2,1,0:T(8,128)(2,1)S(1)}, bf16[4,512,128]{2,1,0:T(8,128)(2,1)}, u32[]{:S(2)}) copy-start(bf16[4,512,128]{2,1,0:T(8,128)(2,1)} %excitation.1) | copy-start | bytes 1572868
  6.0 1.8 %copy-start.2 = (f32[1,512,128]{2,1,0:T(8,128)S(1)}, f32[1,512,128]{2,1,0:T(8,128)}, u32[]{:S(2)}) copy-start(f32[1,512,128]{2,1,0:T(8,128)} %pending.1) | copy-start | bytes 786436
  6.0 1.8 %copy-start.3 = (f32[4,128,128]{2,1,0:T(8,128)S(1)}, f32[4,128,128]{2,1,0:T(8,128)}, u32[]{:S(2)}) copy-start(f32[4,128,128]{2,1,0:T(8,128)} %inverse.1) | copy-start | bytes 786436

commit v2 on v1

v2 whole, which is shorter than its diff:
```python
import functools

import jax
import jax.numpy as jnp
from jax import lax
from jax.experimental import pallas as pl
from jax.experimental.pallas import tpu as pltpu
from jax.sharding import PartitionSpec as P

MESH = pl.DeviceIdType.MESH


def split(value):
    high = value.astype(jnp.bfloat16)
    return high, (value - high.astype(jnp.float32)).astype(jnp.bfloat16)


def collapse_kernel(chunk, cell_ref, block_hbm, high_ref, low_ref, blocks, total, sems):
    columns, block_size = total.shape[1] // total.shape[2], total.shape[2]
    cells = total.shape[0] * columns
    slots = blocks.shape[0]

    def fetch(part):
        place = pl.ds(part * chunk, chunk)
        return pltpu.make_async_copy(block_hbm.at[place], blocks.at[place], sems.at[part])

    for part in range(slots // chunk):
        fetch(part).start()
    total[...] = jnp.zeros_like(total)
    live = cell_ref[slots]

    def add_slot(slot, carry):
        cell = cell_ref[slot]
        row = lax.div(cell, columns)
        start = pl.multiple_of(lax.rem(cell, columns) * block_size, block_size)
        total[row, pl.ds(start, block_size)] += blocks[slot].astype(jnp.float32)
        return carry

    for part in range(slots // chunk):
        fetch(part).wait()
        lax.fori_loop(part * chunk, jnp.clip(live, part * chunk, (part + 1) * chunk), add_slot, 0)

    for cell in range(cells):
        row, column = divmod(cell, columns)
        place = (pl.ds(row * block_size, block_size), pl.ds(column * block_size, block_size))
        high_ref[place], low_ref[place] = split(total[row, pl.ds(column * block_size, block_size)])


def collapse(interaction, slot_row, slot_owner, slot_pos, block_count, row_blocks, rows, capacity):
    slots, block_size, _ = interaction.shape
    columns = rows * capacity
    chunk = max(size for size in range(1, 17) if slots % size == 0)
    away = lax.rem(lax.axis_index("rows") + rows - slot_owner, rows)
    cell = slot_row * columns + away * capacity + slot_pos
    cell = jnp.concatenate([cell, block_count[0]])
    shape = (row_blocks * block_size, columns * block_size)
    vmem = pl.BlockSpec(memory_space=pltpu.VMEM)
    return pl.pallas_call(
        functools.partial(collapse_kernel, chunk),
        in_specs=[pl.BlockSpec(memory_space=pltpu.SMEM), pl.BlockSpec(memory_space=pltpu.HBM)],
        out_specs=[vmem, vmem],
        scratch_shapes=[
            pltpu.VMEM(interaction.shape, jnp.bfloat16),
            pltpu.VMEM((row_blocks, columns * block_size, block_size), jnp.float32),
            pltpu.SemaphoreType.DMA((slots // chunk,)),
        ],
        out_shape=[jax.ShapeDtypeStruct(shape, jnp.bfloat16)] * 2,
        compiler_params=pltpu.CompilerParams(vmem_limit_bytes=32 * 1024 * 1024),
    )(cell, interaction)


def window_kernel(
    rows, lags, steps, row_blocks, capacity,
    excitation, pending, inverse, table, high, low,
    currents, carried,
    solve_high, solve_low, own, sending, landed, handed, summed, asked, asked_scalar,
    row_send, row_recv, lag_send, lag_recv, hand_send, hand_recv, ask_send, ask_recv, local_sem, out_sem, gate,
):
    row = lax.axis_index("rows")
    lag = lax.axis_index("lag")
    block_size = inverse.shape[1]
    depth = capacity * block_size

    barrier = pltpu.get_barrier_semaphore()
    for away in range(1, rows):
        pl.semaphore_signal(barrier, inc=1, device_id=(lax.rem(row + away, rows), lag), device_id_type=MESH)
    for away in range(1, lags):
        pl.semaphore_signal(barrier, inc=1, device_id=(row, lax.rem(lag + away, lags)), device_id_type=MESH)

    own_table = pltpu.make_async_copy(table, asked_scalar.at[rows - 1], local_sem.at[0])
    own_table.start()

    def apply_inverse(block, value):
        return jnp.dot(
            inverse[block], value, precision=lax.Precision.HIGHEST, preferred_element_type=jnp.float32
        )

    def solved_part(step, before):
        parts = []
        for block in range(row_blocks):
            place = pl.ds(block * block_size, block_size)
            parts.append(apply_inverse(block, excitation[step, place].astype(jnp.float32) - before[place]))
        return jnp.concatenate(parts, axis=0)

    def keep_currents(step, value):
        own[step][...] = value.astype(jnp.bfloat16).reshape(own[step].shape)

    @pl.when(lag == 0)
    def _():
        keep_currents(0, solved_part(0, pending.at[0]))

    pl.semaphore_wait(barrier, rows + lags - 2)

    def ask_copy(away):
        target = lax.rem(row + away, rows)
        return pltpu.make_async_remote_copy(
            src_ref=table, dst_ref=asked.at[away - 1], send_sem=ask_send.at[away - 1],
            recv_sem=ask_recv.at[away - 1], device_id=(target, lag), device_id_type=MESH,
        )

    def row_copy(step, away):
        target = lax.rem(row + away, rows)
        return pltpu.make_async_remote_copy(
            src_ref=sending.at[step, away - 1], dst_ref=landed.at[step, away],
            send_sem=row_send.at[step, away - 1], recv_sem=row_recv.at[step, away - 1],
            device_id=(target, lag), device_id_type=MESH,
        )

    def lag_copy(step, target, which):
        return pltpu.make_async_remote_copy(
            src_ref=own[step], dst_ref=own[step],
            send_sem=lag_send.at[step, which], recv_sem=lag_recv.at[step],
            device_id=(row, target), device_id_type=MESH,
        )

    def hand_copy(step):
        source = pending.at[0] if step == 0 else summed.at[step - 1]
        return pltpu.make_async_remote_copy(
            src_ref=source, dst_ref=handed.at[step],
            send_sem=hand_send.at[step], recv_sem=hand_recv.at[step],
            device_id=(row, lax.rem(lag + lags - 1, lags)), device_id_type=MESH,
        )

    def out_copy(step):
        return pltpu.make_async_copy(own[step], currents.at[step], out_sem.at[step])

    def product_of(step, away, first, second):
        place = pl.ds(away * depth, depth)
        values = landed[step, away].reshape(depth, landed.shape[-1])
        return jnp.dot(first[:, place], values, preferred_element_type=jnp.float32) + jnp.dot(
            second[:, place], values, preferred_element_type=jnp.float32
        )

    def product(step, first, second):
        total = product_of(step, 0, first, second)
        for away in range(1, rows):
            row_copy(step, away).wait_recv()
            total += product_of(step, away, first, second)
        return total

    for away in range(1, rows):
        ask_copy(away).start()

    @pl.when(lag > 0)
    def _():
        hand_copy(0).start()

    @pl.when(lag == lags - 1)
    def _():
        handed[...] = jnp.zeros_like(handed)

    to_scalar = pltpu.make_async_copy(asked, asked_scalar.at[pl.ds(0, rows - 1)], local_sem.at[1])
    evens = list(range(2, lags, 2))
    forwards = (lag > 0) & (lax.rem(lag, 2) == 0) & (lag + 1 < lags)

    def send_evens(step):
        for place, target in enumerate(evens):
            lag_copy(step, target, place + 1).start()

    for step in range(steps):
        last = step == steps - 1

        @pl.when(lag > 0)
        def _():
            lag_copy(step, 0, 0).wait_recv()

        if step == 0:
            for away in range(1, rows):
                ask_copy(away).wait_recv()
            to_scalar.start()
            own_table.wait()
            to_scalar.wait()

        @pl.when(forwards)
        def _():
            lag_copy(step, lag + 1, 0).start()

        if last:
            @pl.when(lag == 0)
            def _():
                send_evens(step)
                lag_copy(step, 1, 0).start()

        for away in range(1, rows):
            for entry in range(capacity):
                sending[step, away - 1, entry] = own[step][asked_scalar[rows - away - 1, row, entry]]
        if not last:
            @pl.when(lag == 1)
            def _():
                pl.semaphore_wait(gate.at[step], 1)

        for away in range(1, rows):
            row_copy(step, away).start()

        if not last:
            @pl.when(lag == 0)
            def _():
                lag_copy(step, 1, 0).start()
                send_evens(step)

        out_copy(step).start()
        for entry in range(capacity):
            landed[step, 0, entry] = own[step][asked_scalar[rows - 1, row, entry]]

        if last:
            total = product(step, high, low)

            @pl.when(lag < lags - 1)
            def _():
                hand_copy(step).wait_recv()

            carried[0] = handed[step] + total
            continue

        @pl.when(lag == 0)
        def _():
            if step == 0:
                for block in range(row_blocks):
                    place = pl.ds(block * block_size, block_size)
                    value = high[place].astype(jnp.float32) + low[place].astype(jnp.float32)
                    solve_high[place], solve_low[place] = split(apply_inverse(block, value))
            hand_copy(step).wait_recv()
            base = solved_part(step + 1, handed.at[step])
            for away in range(1, rows):
                row_copy(step, away).wait_send()
            pl.semaphore_signal(gate.at[step], inc=1, device_id=(row, 1), device_id_type=MESH)
            keep_currents(step + 1, base - product(step, solve_high, solve_low))

        @pl.when(lag > 0)
        def _():
            total = product(step, high, low)

            @pl.when(lag < lags - 1)
            def _():
                hand_copy(step).wait_recv()

            summed[step] = handed[step] + total
            hand_copy(step + 1).start()

    for away in range(1, rows):
        ask_copy(away).wait_send()
    for step in range(steps):
        def wait_rows():
            for away in range(1, rows):
                row_copy(step, away).wait_send()

        if step == steps - 1:
            wait_rows()
        else:
            pl.when(lag > 0)(wait_rows)
        out_copy(step).wait()

        @pl.when(lag > 0)
        def _():
            hand_copy(step).wait_send()

        @pl.when(forwards)
        def _():
            lag_copy(step, lag + 1, 0).wait_send()

        @pl.when(lag == 0)
        def _():
            lag_copy(step, 1, 0).wait_send()
            for place, target in enumerate(evens):
                lag_copy(step, target, place + 1).wait_send()


def per_device(
    excitation, pending, inverse, interaction, slot_row, slot_owner, slot_pos, needed, block_count
):
    row_blocks, block_size, _ = inverse.shape
    steps, unknowns, width = excitation.shape
    rows, capacity = needed.shape[1:]
    lags = lax.axis_size("lag")
    high, low = collapse(
        interaction, slot_row, slot_owner, slot_pos, block_count, row_blocks, rows, capacity
    )
    table = jnp.pad(needed[0], ((0, -rows % 8), (0, -capacity % 128)))
    vmem = pl.BlockSpec(memory_space=pltpu.VMEM)
    dma = pltpu.SemaphoreType.DMA
    evens = len(range(2, lags, 2))
    return pl.pallas_call(
        functools.partial(window_kernel, rows, lags, steps, row_blocks, capacity),
        out_shape=[
            jax.ShapeDtypeStruct((steps, row_blocks, block_size, width), jnp.bfloat16),
            jax.ShapeDtypeStruct((1, unknowns, width), jnp.float32),
        ],
        in_specs=[vmem] * 6,
        out_specs=[vmem, vmem],
        scratch_shapes=[
            pltpu.VMEM(high.shape, jnp.bfloat16),
            pltpu.VMEM(low.shape, jnp.bfloat16),
            [pltpu.VMEM((row_blocks, block_size, width), jnp.bfloat16)] * steps,
            pltpu.VMEM((steps, rows - 1, capacity, block_size, width), jnp.bfloat16),
            pltpu.VMEM((steps, rows, capacity, block_size, width), jnp.bfloat16),
            pltpu.VMEM((steps, unknowns, width), jnp.float32),
            pltpu.VMEM((steps, unknowns, width), jnp.float32),
            pltpu.VMEM((rows - 1,) + table.shape, jnp.int32),
            pltpu.SMEM((rows,) + table.shape, jnp.int32),
            dma((steps, rows - 1)),
            dma((steps, rows - 1)),
            dma((steps, evens + 1)),
            dma((steps,)),
            dma((steps,)),
            dma((steps,)),
            dma((rows - 1,)),
            dma((rows - 1,)),
            dma((2,)),
            dma((steps,)),
            pltpu.SemaphoreType.REGULAR((steps,)),
        ],
        compiler_params=pltpu.CompilerParams(
            collective_id=0, has_side_effects=True, vmem_limit_bytes=48 * 1024 * 1024
        ),
    )(excitation, pending, inverse, table, high, low)


def solution(mesh):
    in_specs = (
        P(None, "rows", None),
        P("lag", "rows", None),
        P("rows", None, None),
        P(("rows", "lag"), None, None),
        P(("rows", "lag")),
        P(("rows", "lag")),
        P(("rows", "lag")),
        P(("rows", "lag"), None, None),
        P("rows", "lag"),
    )
    out_specs = (P(None, "rows", None), P("lag", "rows", None))

    def body(*arrays):
        currents, carried = per_device(*arrays)
        return currents.reshape(arrays[0].shape), carried

    return jax.shard_map(body, mesh=mesh, in_specs=in_specs, out_specs=out_specs, check_vma=False)
```

time: 56 us -> 52.8 us (0.943)
  local copies, waits for them, and re-layouts: 6.13 us -> 4.17 us
  Pallas kernels: 47.7 us -> 45.8 us
  other arithmetic: 0.08 us -> 0.78 us
    unnamed x16 -> x10, local copies, waits for them, and re-layouts: 5.36 us -> 3.4 us
    pallas_call x1, Pallas kernels: 46 us -> 44.2 us  [per_device(): pl.pallas_call(functools.partial(window_kernel, rows, lags, steps, row_bl...]
    add x0 -> x1, other arithmetic: none -> 0.7 us  [collapse(): cell = slot_row * columns + away * capacity + slot_pos]
where the time goes in v2:
time: 52.8 us; the launch traced here: 52.1 us
  Pallas kernels  45.8 us (87%)
  local copies, waits for them, and re-layouts  4.17 us (8%)
  between operations  1.33 us (3%)
  other arithmetic  0.78 us (1%)
    pallas_call x1, Pallas kernels, per_device(): pl.pallas_call(functools.partial(window_kernel, rows, lags, steps, row_bl...  44.2 us
    unnamed x10, local copies, waits for them, and re-layouts  3.4 us
    pallas_call x1, Pallas kernels, collapse(): pl.pallas_call(functools.partial(collapse_kernel, chunk), in_specs=[pl.Bl...  1.62 us

profile of v2, /device:TPU:7, one launch (start us, length us, event | category | flops | bytes accessed | tf_op | source)
XLA Modules:
  0.0 52.1 jit_solution(6015360939159787093)
XLA Ops:
  1.3 0.7 %fusion.3 = s32[96]{0:T(128)S(1)} fusion(s32[96]{0:T(128)} %param.15, s32[96]{0:T(128)} %param.14, s32[96]{0:T(128)} %param.13, s32[]{:T(128)S(6)} %add.11), kind=kLoop, calls=%fused_computation.5 | loop fusion | flops 1056 | bytes 1540 | tf_op jit(solution)/shard_map/add | solution.py:54
  2.0 0.1 pad_add_fusion.cell_ref
  2.1 0.8 %copy.11 = s32[4,2]{1,0:T(4,128)S(1)} copy(s32[4,2]{0,1:T(2,128)} %bitcast.5) | data formatting | bytes 64 | tf_op jit(solution)/shard_map/squeeze | solution.py:298
  2.8 0.0 copy-start
  2.8 1.9 %copy-done = bf16[96,128,128]{2,1,0:T(8,128)(2,1)S(1)} copy-done((bf16[96,128,128]{2,1,0:T(8,128)(2,1)S(1)}, bf16[96,128,128]{2,1,0:T(8,128)(2,1)}, u32[]{:S(2)}) %copy-start) | copy-done | bytes 3145752
  4.7 0.0 copy-start.1
  4.7 0.0 copy-start.2
  4.7 0.0 copy-start.3
  4.7 1.6 %shard_map.104 = (bf16[512,1024]{1,0:T(8,128)(2,1)S(1)}, bf16[512,1024]{1,0:T(8,128)(2,1)S(1)}) custom-call(s32[97]{0:T(128)S(1)} %pad_add_fusion.cell_ref, bf16[96,128,128]{2,1,0:T(8,128)(2,1)S(1)} %copy-done), custom_call_target="tpu_custom_call" | custom-call | tf_op jit(solution)/shard_map/pallas_call | solution.py:58
  6.4 0.0 copy-done.1
  6.4 0.0 copy-done.2
  6.4 0.0 copy-done.3
  6.4 44.2 %shard_map.105 = (bf16[4,4,128,128]{3,2,1,0:T(8,128)(2,1)S(1)}, f32[1,512,128]{2,1,0:T(8,128)S(1)}) custom-call(bf16[4,512,128]{2,1,0:T(8,128)(2,1)S(1)} %copy-done.1, f32[1,512,128]{2,1,0:T(8,128)S(1)} %copy-done.2, f32[4,128,128]{2,1,0:T(8,128)S(1)} %copy-done.3, s32[8,128]{1,0:T(8,128)S(1)} %pad.4.table, bf16[512,1024]{1,0:T(8,128)(2,1)S(1)} %get-tuple-element.6.high, ...), custom_call_target="tpu_custom_call" | custom-call | tf_op jit(solution)/shard_map/pallas_call | solution.py:302
  50.6 0.8 %copy.15 = bf16[4,512,128]{2,1,0:T(8,128)(2,1)} copy(bf16[4,512,128]{2,1,0:T(8,128)(2,1)S(1)} %bitcast.4) | data formatting | bytes 1048576
  51.4 0.7 %copy.16 = f32[1,512,128]{2,1,0:T(8,128)} copy(f32[1,512,128]{2,1,0:T(8,128)S(1)} %get-tuple-element.13) | data formatting | bytes 524288
  (1 shorter events, 0.0 us)
Async XLA Ops:
  2.8 1.9 %copy-start = (bf16[96,128,128]{2,1,0:T(8,128)(2,1)S(1)}, bf16[96,128,128]{2,1,0:T(8,128)(2,1)}, u32[]{:S(2)}) copy-start(bf16[96,128,128]{2,1,0:T(8,128)(2,1)} %block_hbm.1) | copy-start | bytes 9437188
  4.7 1.6 %copy-start.1 = (bf16[4,512,128]{2,1,0:T(8,128)(2,1)S(1)}, bf16[4,512,128]{2,1,0:T(8,128)(2,1)}, u32[]{:S(2)}) copy-start(bf16[4,512,128]{2,1,0:T(8,128)(2,1)} %excitation.1) | copy-start | bytes 1572868
  4.7 1.6 %copy-start.2 = (f32[1,512,128]{2,1,0:T(8,128)S(1)}, f32[1,512,128]{2,1,0:T(8,128)}, u32[]{:S(2)}) copy-start(f32[1,512,128]{2,1,0:T(8,128)} %pending.1) | copy-start | bytes 786436
  4.7 1.7 %copy-start.3 = (f32[4,128,128]{2,1,0:T(8,128)S(1)}, f32[4,128,128]{2,1,0:T(8,128)}, u32[]{:S(2)}) copy-start(f32[4,128,128]{2,1,0:T(8,128)} %inverse.1) | copy-start | bytes 786436

commit v3 on v2

--- a/solution.py
+++ b/solution.py
@@ -65,7 +65,7 @@
             pltpu.SemaphoreType.DMA((slots // chunk,)),
         ],
         out_shape=[jax.ShapeDtypeStruct(shape, jnp.bfloat16)] * 2,
-        compiler_params=pltpu.CompilerParams(vmem_limit_bytes=32 * 1024 * 1024),
+        compiler_params=pltpu.CompilerParams(vmem_limit_bytes=60 * 1024 * 1024),
     )(cell, interaction)
 
 
@@ -80,6 +80,11 @@
     lag = lax.axis_index("lag")
     block_size = inverse.shape[1]
     depth = capacity * block_size
+    pieces = [len(own[step]) for step in range(steps)]
+
+    def rows_of(step, piece):
+        size = block_size // pieces[step]
+        return pl.ds(piece * size, size)
 
     barrier = pltpu.get_barrier_semaphore()
     for away in range(1, rows):
@@ -103,7 +108,10 @@
         return jnp.concatenate(parts, axis=0)
 
     def keep_currents(step, value):
-        own[step][...] = value.astype(jnp.bfloat16).reshape(own[step].shape)
+        value = value.astype(jnp.bfloat16).reshape(row_blocks, block_size, value.shape[-1])
+        size = block_size // pieces[step]
+        for piece in range(pieces[step]):
+            own[step][piece][...] = value[:, piece * size : (piece + 1) * size]
 
     @pl.when(lag == 0)
     def _():
@@ -118,18 +126,19 @@
             recv_sem=ask_recv.at[away - 1], device_id=(target, lag), device_id_type=MESH,
         )
 
-    def row_copy(step, away):
+    def row_copy(step, piece, away):
         target = lax.rem(row + away, rows)
         return pltpu.make_async_remote_copy(
-            src_ref=sending.at[step, away - 1], dst_ref=landed.at[step, away],
-            send_sem=row_send.at[step, away - 1], recv_sem=row_recv.at[step, away - 1],
+            src_ref=sending.at[step, away - 1, :, rows_of(step, piece)],
+            dst_ref=landed.at[step, away, :, rows_of(step, piece)],
+            send_sem=row_send.at[step, piece, away - 1], recv_sem=row_recv.at[step, piece, away - 1],
             device_id=(target, lag), device_id_type=MESH,
         )
 
-    def lag_copy(step, target, which):
+    def lag_copy(step, piece, target, which):
         return pltpu.make_async_remote_copy(
-            src_ref=own[step], dst_ref=own[step],
-            send_sem=lag_send.at[step, which], recv_sem=lag_recv.at[step],
+            src_ref=own[step][piece], dst_ref=own[step][piece],
+            send_sem=lag_send.at[step, piece, which], recv_sem=lag_recv.at[step, piece],
             device_id=(row, target), device_id_type=MESH,
         )
 
@@ -141,8 +150,10 @@
             device_id=(row, lax.rem(lag + lags - 1, lags)), device_id_type=MESH,
         )
 
-    def out_copy(step):
-        return pltpu.make_async_copy(own[step], currents.at[step], out_sem.at[step])
+    def out_copy(step, piece):
+        return pltpu.make_async_copy(
+            own[step][piece], currents.at[step, :, rows_of(step, piece)], out_sem.at[step, piece]
+        )
 
     def product_of(step, away, first, second):
         place = pl.ds(away * depth, depth)
@@ -154,7 +165,8 @@
     def product(step, first, second):
         total = product_of(step, 0, first, second)
         for away in range(1, rows):
-            row_copy(step, away).wait_recv()
+            for piece in range(pieces[step]):
+                row_copy(step, piece, away).wait_recv()
             total += product_of(step, away, first, second)
         return total
 
@@ -173,54 +185,58 @@
     evens = list(range(2, lags, 2))
     forwards = (lag > 0) & (lax.rem(lag, 2) == 0) & (lag + 1 < lags)
 
-    def send_evens(step):
+    def send_evens(step, piece):
         for place, target in enumerate(evens):
-            lag_copy(step, target, place + 1).start()
+            lag_copy(step, piece, target, place + 1).start()
 
     for step in range(steps):
         last = step == steps - 1
 
-        @pl.when(lag > 0)
-        def _():
-            lag_copy(step, 0, 0).wait_recv()
-
-        if step == 0:
-            for away in range(1, rows):
-                ask_copy(away).wait_recv()
-            to_scalar.start()
-            own_table.wait()
-            to_scalar.wait()
-
-        @pl.when(forwards)
-        def _():
-            lag_copy(step, lag + 1, 0).start()
-
         if last:
             @pl.when(lag == 0)
             def _():
-                send_evens(step)
-                lag_copy(step, 1, 0).start()
-
-        for away in range(1, rows):
+                for piece in range(pieces[step]):
+                    send_evens(step, piece)
+                    lag_copy(step, piece, 1, 0).start()
+
+        for piece in range(pieces[step]):
+            @pl.when(lag > 0)
+            def _():
+                lag_copy(step, piece, 0, 0).wait_recv()
+
+            if step == 0:
+                for away in range(1, rows):
+                    ask_copy(away).wait_recv()
+                to_scalar.start()
+                own_table.wait()
+                to_scalar.wait()
+
+            @pl.when(forwards)
+            def _():
+                lag_copy(step, piece, lag + 1, 0).start()
+
+            place = rows_of(step, piece)
+            for away in range(1, rows):
+                for entry in range(capacity):
+                    block = asked_scalar[rows - away - 1, row, entry]
+                    sending[step, away - 1, entry, place] = own[step][piece][block]
+            if not last:
+                @pl.when(lag == 1)
+                def _():
+                    pl.semaphore_wait(gate.at[step], 1)
+
+            for away in range(1, rows):
+                row_copy(step, piece, away).start()
+
+            if not last:
+                @pl.when(lag == 0)
+                def _():
+                    lag_copy(step, piece, 1, 0).start()
+                    send_evens(step, piece)
+
+            out_copy(step, piece).start()
             for entry in range(capacity):
-                sending[step, away - 1, entry] = own[step][asked_scalar[rows - away - 1, row, entry]]
-        if not last:
-            @pl.when(lag == 1)
-            def _():
-                pl.semaphore_wait(gate.at[step], 1)
-
-        for away in range(1, rows):
-            row_copy(step, away).start()
-
-        if not last:
-            @pl.when(lag == 0)
-            def _():
-                lag_copy(step, 1, 0).start()
-                send_evens(step)
-
-        out_copy(step).start()
-        for entry in range(capacity):
-            landed[step, 0, entry] = own[step][asked_scalar[rows - 1, row, entry]]
+                landed[step, 0, entry, place] = own[step][piece][asked_scalar[rows - 1, row, entry]]
 
         if last:
             total = product(step, high, low)
@@ -239,11 +255,11 @@
                     place = pl.ds(block * block_size, block_size)
                     value = high[place].astype(jnp.float32) + low[place].astype(jnp.float32)
                     solve_high[place], solve_low[place] = split(apply_inverse(block, value))
+            for away in range(1, rows):
+                row_copy(step, 0, away).wait_send()
+            pl.semaphore_signal(gate.at[step], inc=1, device_id=(row, 1), device_id_type=MESH)
             hand_copy(step).wait_recv()
             base = solved_part(step + 1, handed.at[step])
-            for away in range(1, rows):
-                row_copy(step, away).wait_send()
-            pl.semaphore_signal(gate.at[step], inc=1, device_id=(row, 1), device_id_type=MESH)
             keep_currents(step + 1, base - product(step, solve_high, solve_low))
 
         @pl.when(lag > 0)
@@ -260,29 +276,30 @@
     for away in range(1, rows):
         ask_copy(away).wait_send()
     for step in range(steps):
-        def wait_rows():
-            for away in range(1, rows):
-                row_copy(step, away).wait_send()
-
-        if step == steps - 1:
-            wait_rows()
-        else:
-            pl.when(lag > 0)(wait_rows)
-        out_copy(step).wait()
-
         @pl.when(lag > 0)
         def _():
             hand_copy(step).wait_send()
 
-        @pl.when(forwards)
-        def _():
-            lag_copy(step, lag + 1, 0).wait_send()
-
-        @pl.when(lag == 0)
-        def _():
-            lag_copy(step, 1, 0).wait_send()
-            for place, target in enumerate(evens):
-                lag_copy(step, target, place + 1).wait_send()
+        for piece in range(pieces[step]):
+            def wait_rows():
+                for away in range(1, rows):
+                    row_copy(step, piece, away).wait_send()
+
+            if step == steps - 1:
+                wait_rows()
+            else:
+                pl.when(lag > 0)(wait_rows)
+            out_copy(step, piece).wait()
+
+            @pl.when(forwards)
+            def _():
+                lag_copy(step, piece, lag + 1, 0).wait_send()
+
+            @pl.when(lag == 0)
+            def _():
+                lag_copy(step, piece, 1, 0).wait_send()
+                for place, target in enumerate(evens):
+                    lag_copy(step, piece, target, place + 1).wait_send()
 
 
 def per_device(
@@ -299,6 +316,7 @@
     vmem = pl.BlockSpec(memory_space=pltpu.VMEM)
     dma = pltpu.SemaphoreType.DMA
     evens = len(range(2, lags, 2))
+    tail = 2 if block_size % 32 == 0 else 1
     return pl.pallas_call(
         functools.partial(window_kernel, rows, lags, steps, row_blocks, capacity),
         out_shape=[
@@ -310,23 +328,26 @@
         scratch_shapes=[
             pltpu.VMEM(high.shape, jnp.bfloat16),
             pltpu.VMEM(low.shape, jnp.bfloat16),
-            [pltpu.VMEM((row_blocks, block_size, width), jnp.bfloat16)] * steps,
+            [
+                [pltpu.VMEM((row_blocks, block_size // cut, width), jnp.bfloat16)] * cut
+                for cut in [1] * (steps - 1) + [tail]
+            ],
             pltpu.VMEM((steps, rows - 1, capacity, block_size, width), jnp.bfloat16),
             pltpu.VMEM((steps, rows, capacity, block_size, width), jnp.bfloat16),
             pltpu.VMEM((steps, unknowns, width), jnp.float32),
             pltpu.VMEM((steps, unknowns, width), jnp.float32),
             pltpu.VMEM((rows - 1,) + table.shape, jnp.int32),
             pltpu.SMEM((rows,) + table.shape, jnp.int32),
-            dma((steps, rows - 1)),
-            dma((steps, rows - 1)),
-            dma((steps, evens + 1)),
-            dma((steps,)),
+            dma((steps, tail, rows - 1)),
+            dma((steps, tail, rows - 1)),
+            dma((steps, tail, evens + 1)),
+            dma((steps, tail)),
             dma((steps,)),
             dma((steps,)),
             dma((rows - 1,)),
             dma((rows - 1,)),
             dma((2,)),
-            dma((steps,)),
+            dma((steps, tail)),
             pltpu.SemaphoreType.REGULAR((steps,)),
         ],
         compiler_params=pltpu.CompilerParams(

time: 52.8 us -> 57.8 us (1.095)
  Pallas kernels: 45.8 us -> 49.6 us
    pallas_call x1, Pallas kernels: 1.62 us -> 4.44 us  [collapse(): pl.pallas_call(functools.partial(collapse_kernel, chunk), in_specs=[pl.Bl...]
    pallas_call x1, Pallas kernels: 44.2 us -> 45.2 us  [per_device(): pl.pallas_call(functools.partial(window_kernel, rows, lags, steps, row_bl...]
    unnamed x10 -> x12, local copies, waits for them, and re-layouts: 3.4 us -> 3.95 us
where the time goes in v3:
time: 57.8 us; the launch traced here: 57.1 us
  Pallas kernels  49.6 us (86%)
  local copies, waits for them, and re-layouts  4.72 us (8%)
  between operations  1.44 us (2%)
  other arithmetic  1.29 us (2%)
    pallas_call x1, Pallas kernels, per_device(): pl.pallas_call(functools.partial(window_kernel, rows, lags, steps, row_bl...  45.2 us
    pallas_call x1, Pallas kernels, collapse(): pl.pallas_call(functools.partial(collapse_kernel, chunk), in_specs=[pl.Bl...  4.44 us
    unnamed x12, local copies, waits for them, and re-layouts  3.95 us

profile of v3, /device:TPU:7, one launch (start us, length us, event | category | flops | bytes accessed | tf_op | source)
XLA Modules:
  0.0 57.1 jit_solution(13085886586913625141)
XLA Ops:
  0.6 0.0 copy-start.4
  0.6 0.0 copy-start.3
  0.7 0.0 copy-start.2
  1.4 0.7 %fusion.3 = s32[96]{0:T(128)S(1)} fusion(s32[96]{0:T(128)} %param.15, s32[96]{0:T(128)} %param.14, s32[96]{0:T(128)} %param.13, s32[]{:T(128)S(6)} %add.11), kind=kLoop, calls=%fused_computation.5 | loop fusion | flops 1056 | bytes 1540 | tf_op jit(solution)/shard_map/add | solution.py:54
  2.1 0.6 %pad_add_fusion.cell_ref = s32[97]{0:T(128)} fusion(s32[1]{0:T(128)} %bitcast.3, s32[96]{0:T(128)S(1)} %fusion.3), kind=kLoop, calls=%fused_computation.6 | loop fusion | flops 97 | bytes 776 | tf_op jit(solution)/shard_map/concatenate | solution.py:55
  2.7 0.8 %copy.11 = s32[4,2]{1,0:T(4,128)S(1)} copy(s32[4,2]{0,1:T(2,128)} %bitcast.5) | data formatting | bytes 64 | tf_op jit(solution)/shard_map/squeeze | solution.py:315
  3.5 4.4 %shard_map.104 = (bf16[512,1024]{1,0:T(8,128)(2,1)}, bf16[512,1024]{1,0:T(8,128)(2,1)}) custom-call(s32[97]{0:T(128)} %pad_add_fusion.cell_ref, bf16[96,128,128]{2,1,0:T(8,128)(2,1)} %block_hbm.1), custom_call_target="tpu_custom_call" | custom-call | tf_op jit(solution)/shard_map/pallas_call | solution.py:58
  7.9 0.0 copy-done.4
  7.9 0.0 copy-done.3
  7.9 0.0 copy-done.2
  7.9 0.0 copy-start
  7.9 1.2 %copy-done = bf16[512,1024]{1,0:T(8,128)(2,1)S(1)} copy-done((bf16[512,1024]{1,0:T(8,128)(2,1)S(1)}, bf16[512,1024]{1,0:T(8,128)(2,1)}, u32[]{:S(2)}) %copy-start) | copy-done | bytes 1048600
  9.2 0.0 copy-start.1
  9.2 1.2 %copy-done.1 = bf16[512,1024]{1,0:T(8,128)(2,1)S(1)} copy-done((bf16[512,1024]{1,0:T(8,128)(2,1)S(1)}, bf16[512,1024]{1,0:T(8,128)(2,1)}, u32[]{:S(2)}) %copy-start.1) | copy-done | bytes 1048600
  10.4 45.2 %shard_map.105 = (bf16[4,4,128,128]{3,2,1,0:T(8,128)(2,1)S(1)}, f32[1,512,128]{2,1,0:T(8,128)S(1)}) custom-call(bf16[4,512,128]{2,1,0:T(8,128)(2,1)S(1)} %copy-done.2, f32[1,512,128]{2,1,0:T(8,128)S(1)} %copy-done.3, f32[4,128,128]{2,1,0:T(8,128)S(1)} %copy-done.4, s32[8,128]{1,0:T(8,128)S(1)} %pad.4.table, bf16[512,1024]{1,0:T(8,128)(2,1)S(1)} %copy-done, ...), custom_call_target="tpu_custom_call" | custom-call | tf_op jit(solution)/shard_map/pallas_call | solution.py:320
  55.6 0.8 %copy.15 = bf16[4,512,128]{2,1,0:T(8,128)(2,1)} copy(bf16[4,512,128]{2,1,0:T(8,128)(2,1)S(1)} %bitcast.4) | data formatting | bytes 1048576
  56.4 0.7 %copy.16 = f32[1,512,128]{2,1,0:T(8,128)} copy(f32[1,512,128]{2,1,0:T(8,128)S(1)} %get-tuple-element.13) | data formatting | bytes 524288
  (1 shorter events, 0.0 us)
Async XLA Ops:
  0.6 7.3 %copy-start.4 = (f32[4,128,128]{2,1,0:T(8,128)S(1)}, f32[4,128,128]{2,1,0:T(8,128)}, u32[]{:S(2)}) copy-start(f32[4,128,128]{2,1,0:T(8,128)} %inverse.1) | copy-start | bytes 786436
  0.6 7.3 %copy-start.3 = (f32[1,512,128]{2,1,0:T(8,128)S(1)}, f32[1,512,128]{2,1,0:T(8,128)}, u32[]{:S(2)}) copy-start(f32[1,512,128]{2,1,0:T(8,128)} %pending.1) | copy-start | bytes 786436
  0.7 7.3 %copy-start.2 = (bf16[4,512,128]{2,1,0:T(8,128)(2,1)S(1)}, bf16[4,512,128]{2,1,0:T(8,128)(2,1)}, u32[]{:S(2)}) copy-start(bf16[4,512,128]{2,1,0:T(8,128)(2,1)} %excitation.1) | copy-start | bytes 1572868
  7.9 1.2 %copy-start = (bf16[512,1024]{1,0:T(8,128)(2,1)S(1)}, bf16[512,1024]{1,0:T(8,128)(2,1)}, u32[]{:S(2)}) copy-start(bf16[512,1024]{1,0:T(8,128)(2,1)} %get-tuple-element.6.high) | copy-start | bytes 3145732
  9.2 1.2 %copy-start.1 = (bf16[512,1024]{1,0:T(8,128)(2,1)S(1)}, bf16[512,1024]{1,0:T(8,128)(2,1)}, u32[]{:S(2)}) copy-start(bf16[512,1024]{1,0:T(8,128)(2,1)} %get-tuple-element.7.low) | copy-start | bytes 3145732

commit v4 on v2

--- a/solution.py
+++ b/solution.py
@@ -73,13 +73,29 @@
     rows, lags, steps, row_blocks, capacity,
     excitation, pending, inverse, table, high, low,
     currents, carried,
-    solve_high, solve_low, own, sending, landed, handed, summed, asked, asked_scalar,
+    solve_high, solve_low, own, whole, sending, landed, handed, summed, asked, asked_scalar,
     row_send, row_recv, lag_send, lag_recv, hand_send, hand_recv, ask_send, ask_recv, local_sem, out_sem, gate,
+    spread_send, along_send, gather_send, gather_recv, odd_send, odd_recv,
 ):
     row = lax.axis_index("rows")
     lag = lax.axis_index("lag")
     block_size = inverse.shape[1]
     depth = capacity * block_size
+    final = steps - 1
+    own = list(own) + [whole[0]]
+    pairs = lags // 2
+    pair = lax.div(lag, 2)
+    even = lax.rem(lag, 2) == 0
+    cuts = whole[0].shape[1]
+    each = row_blocks * cuts // pairs
+
+    def picked(ref, index):
+        return ref[index].reshape(block_size, ref.shape[-1])
+
+    def piece_of(ref, index):
+        if cuts > 1:
+            return ref.at[lax.div(index, cuts), lax.rem(index, cuts)]
+        return ref.at[pl.ds(index * each, each)]
 
     barrier = pltpu.get_barrier_semaphore()
     for away in range(1, rows):
@@ -177,9 +193,7 @@
         for place, target in enumerate(evens):
             lag_copy(step, target, place + 1).start()
 
-    for step in range(steps):
-        last = step == steps - 1
-
+    for step in range(final):
         @pl.when(lag > 0)
         def _():
             lag_copy(step, 0, 0).wait_recv()
@@ -195,42 +209,25 @@
         def _():
             lag_copy(step, lag + 1, 0).start()
 
-        if last:
-            @pl.when(lag == 0)
-            def _():
-                send_evens(step)
-                lag_copy(step, 1, 0).start()
-
         for away in range(1, rows):
             for entry in range(capacity):
-                sending[step, away - 1, entry] = own[step][asked_scalar[rows - away - 1, row, entry]]
-        if not last:
-            @pl.when(lag == 1)
-            def _():
-                pl.semaphore_wait(gate.at[step], 1)
+                sending[step, away - 1, entry] = picked(own[step], asked_scalar[rows - away - 1, row, entry])
+
+        @pl.when(lag == 1)
+        def _():
+            pl.semaphore_wait(gate.at[step], 1)
 
         for away in range(1, rows):
             row_copy(step, away).start()
 
-        if not last:
-            @pl.when(lag == 0)
-            def _():
-                lag_copy(step, 1, 0).start()
-                send_evens(step)
+        @pl.when(lag == 0)
+        def _():
+            lag_copy(step, 1, 0).start()
+            send_evens(step)
 
         out_copy(step).start()
         for entry in range(capacity):
-            landed[step, 0, entry] = own[step][asked_scalar[rows - 1, row, entry]]
-
-        if last:
-            total = product(step, high, low)
-
-            @pl.when(lag < lags - 1)
-            def _():
-                hand_copy(step).wait_recv()
-
-            carried[0] = handed[step] + total
-            continue
+            landed[step, 0, entry] = picked(own[step], asked_scalar[rows - 1, row, entry])
 
         @pl.when(lag == 0)
         def _():
@@ -239,11 +236,11 @@
                     place = pl.ds(block * block_size, block_size)
                     value = high[place].astype(jnp.float32) + low[place].astype(jnp.float32)
                     solve_high[place], solve_low[place] = split(apply_inverse(block, value))
-            hand_copy(step).wait_recv()
-            base = solved_part(step + 1, handed.at[step])
             for away in range(1, rows):
                 row_copy(step, away).wait_send()
             pl.semaphore_signal(gate.at[step], inc=1, device_id=(row, 1), device_id_type=MESH)
+            hand_copy(step).wait_recv()
+            base = solved_part(step + 1, handed.at[step])
             keep_currents(step + 1, base - product(step, solve_high, solve_low))
 
         @pl.when(lag > 0)
@@ -257,32 +254,128 @@
             summed[step] = handed[step] + total
             hand_copy(step + 1).start()
 
+    def spread_copy(target):
+        return pltpu.make_async_remote_copy(
+            src_ref=piece_of(whole[0], target), dst_ref=piece_of(whole[0], target),
+            send_sem=spread_send.at[target], recv_sem=gather_recv.at[0, target],
+            device_id=(row, 2 * target), device_id_type=MESH,
+        )
+
+    def along_copy(away):
+        return pltpu.make_async_remote_copy(
+            src_ref=piece_of(whole[0], pair), dst_ref=piece_of(whole[away], pair),
+            send_sem=along_send.at[away - 1], recv_sem=gather_recv.at[away, pair],
+            device_id=(lax.rem(row + away, rows), lag), device_id_type=MESH,
+        )
+
+    def gather_copy(away, turn):
+        return pltpu.make_async_remote_copy(
+            src_ref=piece_of(whole[away], pair), dst_ref=piece_of(whole[away], pair),
+            send_sem=gather_send.at[away, turn - 1], recv_sem=gather_recv.at[away, pair],
+            device_id=(row, 2 * lax.rem(pair + turn, pairs)), device_id_type=MESH,
+        )
+
+    def arrival(away, source):
+        return pltpu.make_async_remote_copy(
+            src_ref=piece_of(whole[away], source), dst_ref=piece_of(whole[away], source),
+            send_sem=gather_send.at[away, 0], recv_sem=gather_recv.at[away, source],
+            device_id=(row, lax.rem(lag + 2, lags)), device_id_type=MESH,
+        )
+
+    def odd_copy(away):
+        return pltpu.make_async_remote_copy(
+            src_ref=whole[away], dst_ref=whole[away],
+            send_sem=odd_send.at[away], recv_sem=odd_recv.at[away],
+            device_id=(row, lax.rem(lag + 1, lags)), device_id_type=MESH,
+        )
+
+    @pl.when(lag == 0)
+    def _():
+        for target in range(1, pairs):
+            spread_copy(target).start()
+        odd_copy(0).start()
+
+    @pl.when(even)
+    def _():
+        @pl.when(lag > 0)
+        def _():
+            arrival(0, pair).wait_recv()
+
+        for away in range(1, rows):
+            along_copy(away).start()
+        for turn in range(1, pairs):
+            @pl.when(lax.rem(pair + turn, pairs) > 0)
+            def _():
+                gather_copy(0, turn).start()
+        for away in range(1, rows):
+            arrival(away, pair).wait_recv()
+            for turn in range(1, pairs):
+                gather_copy(away, turn).start()
+
+    total = None
+    for away in range(rows):
+        @pl.when(even if away > 0 else even & (lag > 0))
+        def _():
+            for turn in range(1, pairs):
+                arrival(away, lax.rem(pair + turn, pairs)).wait_recv()
+            odd_copy(away).start()
+
+        @pl.when(jnp.logical_not(even))
+        def _():
+            odd_copy(away).wait_recv()
+
+        if away == 0:
+            out_copy(final).start()
+        source = lax.rem(row + rows - away, rows)
+        for entry in range(capacity):
+            landed[final, away, entry] = picked(whole[away], asked_scalar[rows - 1, source, entry])
+        part = product_of(final, away, high, low)
+        total = part if total is None else total + part
+
+    @pl.when(lag < lags - 1)
+    def _():
+        hand_copy(final).wait_recv()
+
+    carried[0] = handed[final] + total
+
     for away in range(1, rows):
         ask_copy(away).wait_send()
     for step in range(steps):
-        def wait_rows():
-            for away in range(1, rows):
-                row_copy(step, away).wait_send()
-
-        if step == steps - 1:
-            wait_rows()
-        else:
-            pl.when(lag > 0)(wait_rows)
         out_copy(step).wait()
 
         @pl.when(lag > 0)
         def _():
             hand_copy(step).wait_send()
-
-        @pl.when(forwards)
-        def _():
-            lag_copy(step, lag + 1, 0).wait_send()
-
-        @pl.when(lag == 0)
-        def _():
-            lag_copy(step, 1, 0).wait_send()
-            for place, target in enumerate(evens):
-                lag_copy(step, target, place + 1).wait_send()
+            if step < final:
+                for away in range(1, rows):
+                    row_copy(step, away).wait_send()
+
+        if step < final:
+            @pl.when(forwards)
+            def _():
+                lag_copy(step, lag + 1, 0).wait_send()
+
+            @pl.when(lag == 0)
+            def _():
+                lag_copy(step, 1, 0).wait_send()
+                for place, target in enumerate(evens):
+                    lag_copy(step, target, place + 1).wait_send()
+
+    @pl.when(lag == 0)
+    def _():
+        for target in range(1, pairs):
+            spread_copy(target).wait_send()
+
+    @pl.when(even)
+    def _():
+        for away in range(1, rows):
+            along_copy(away).wait_send()
+        for away in range(rows):
+            odd_copy(away).wait_send()
+            for turn in range(1, pairs):
+                @pl.when((lax.rem(pair + turn, pairs) > 0) | (away > 0))
+                def _():
+                    gather_copy(away, turn).wait_send()
 
 
 def per_device(
@@ -299,10 +392,12 @@
     vmem = pl.BlockSpec(memory_space=pltpu.VMEM)
     dma = pltpu.SemaphoreType.DMA
     evens = len(range(2, lags, 2))
+    cuts = max(1, lags // 2 // row_blocks)
+    shape = (row_blocks, cuts, block_size // cuts, width)
     return pl.pallas_call(
         functools.partial(window_kernel, rows, lags, steps, row_blocks, capacity),
         out_shape=[
-            jax.ShapeDtypeStruct((steps, row_blocks, block_size, width), jnp.bfloat16),
+            jax.ShapeDtypeStruct((steps,) + shape, jnp.bfloat16),
             jax.ShapeDtypeStruct((1, unknowns, width), jnp.float32),
         ],
         in_specs=[vmem] * 6,
@@ -310,7 +405,8 @@
         scratch_shapes=[
             pltpu.VMEM(high.shape, jnp.bfloat16),
             pltpu.VMEM(low.shape, jnp.bfloat16),
-            [pltpu.VMEM((row_blocks, block_size, width), jnp.bfloat16)] * steps,
+            [pltpu.VMEM(shape, jnp.bfloat16)] * (steps - 1),
+            [pltpu.VMEM(shape, jnp.bfloat16)] * rows,
             pltpu.VMEM((steps, rows - 1, capacity, block_size, width), jnp.bfloat16),
             pltpu.VMEM((steps, rows, capacity, block_size, width), jnp.bfloat16),
             pltpu.VMEM((steps, unknowns, width), jnp.float32),
@@ -328,6 +424,12 @@
             dma((2,)),
             dma((steps,)),
             pltpu.SemaphoreType.REGULAR((steps,)),
+            dma((lags // 2,)),
+            dma((rows,)),
+            dma((rows, lags // 2)),
+            dma((rows, lags // 2)),
+            dma((rows,)),
+            dma((rows,)),
         ],
         compiler_params=pltpu.CompilerParams(
             collective_id=0, has_side_effects=True, vmem_limit_bytes=48 * 1024 * 1024

time: 52.8 us -> 58.4 us (1.11)
  the two profiles are of different devices: /device:TPU:7 before, /device:TPU:1 now
where the time goes in v4:
time: 58.4 us; the launch traced here: 58.3 us
  Pallas kernels  52 us (89%)
  local copies, waits for them, and re-layouts  4.17 us (7%)
  between operations  1.33 us (2%)
  other arithmetic  0.78 us (1%)
    pallas_call x1, Pallas kernels, per_device(): pl.pallas_call(functools.partial(window_kernel, rows, lags, steps, row_bl...  49.8 us
    unnamed x10, local copies, waits for them, and re-layouts  3.4 us
    pallas_call x1, Pallas kernels, collapse(): pl.pallas_call(functools.partial(collapse_kernel, chunk), in_specs=[pl.Bl...  2.22 us

profile of v4, /device:TPU:1, one launch (start us, length us, event | category | flops | bytes accessed | tf_op | source)
XLA Modules:
  0.0 58.3 jit_solution(11470076491801869452)
XLA Ops:
  1.3 0.7 %fusion.3 = s32[96]{0:T(128)S(1)} fusion(s32[96]{0:T(128)} %param.15, s32[96]{0:T(128)} %param.14, s32[96]{0:T(128)} %param.13, s32[]{:T(128)S(6)} %add.11), kind=kLoop, calls=%fused_computation.5 | loop fusion | flops 1056 | bytes 1540 | tf_op jit(solution)/shard_map/add | solution.py:54
  2.0 0.1 pad_add_fusion.cell_ref
  2.1 0.8 %copy.11 = s32[4,2]{1,0:T(4,128)S(1)} copy(s32[4,2]{0,1:T(2,128)} %bitcast.5) | data formatting | bytes 64 | tf_op jit(solution)/shard_map/squeeze | solution.py:391
  2.8 0.0 copy-start
  2.8 1.9 %copy-done = bf16[96,128,128]{2,1,0:T(8,128)(2,1)S(1)} copy-done((bf16[96,128,128]{2,1,0:T(8,128)(2,1)S(1)}, bf16[96,128,128]{2,1,0:T(8,128)(2,1)}, u32[]{:S(2)}) %copy-start) | copy-done | bytes 3145752
  4.7 0.0 copy-start.1
  4.7 0.0 copy-start.2
  4.7 0.0 copy-start.3
  4.7 2.2 %shard_map.104 = (bf16[512,1024]{1,0:T(8,128)(2,1)S(1)}, bf16[512,1024]{1,0:T(8,128)(2,1)S(1)}) custom-call(s32[97]{0:T(128)S(1)} %pad_add_fusion.cell_ref, bf16[96,128,128]{2,1,0:T(8,128)(2,1)S(1)} %copy-done), custom_call_target="tpu_custom_call" | custom-call | tf_op jit(solution)/shard_map/pallas_call | solution.py:58
  7.0 0.0 copy-done.1
  7.0 0.0 copy-done.2
  7.0 0.0 copy-done.3
  7.0 49.8 %shard_map.105 = (bf16[4,4,1,128,128]{4,3,2,1,0:T(8,128)(2,1)S(1)}, f32[1,512,128]{2,1,0:T(8,128)S(1)}) custom-call(bf16[4,512,128]{2,1,0:T(8,128)(2,1)S(1)} %copy-done.1, f32[1,512,128]{2,1,0:T(8,128)S(1)} %copy-done.2, f32[4,128,128]{2,1,0:T(8,128)S(1)} %copy-done.3, s32[8,128]{1,0:T(8,128)S(1)} %pad.4.table, bf16[512,1024]{1,0:T(8,128)(2,1)S(1)} %get-tuple-element.6.high, ...), custom_call_target="tpu_custom_call" | custom-call | tf_op jit(solution)/shard_map/pallas_call | solution.py:397
  56.8 0.8 %copy.15 = bf16[4,512,128]{2,1,0:T(8,128)(2,1)} copy(bf16[4,512,128]{2,1,0:T(8,128)(2,1)S(1)} %bitcast.4) | data formatting | bytes 1048576
  57.6 0.7 %copy.16 = f32[1,512,128]{2,1,0:T(8,128)} copy(f32[1,512,128]{2,1,0:T(8,128)S(1)} %get-tuple-element.13) | data formatting | bytes 524288
  (1 shorter events, 0.0 us)
Async XLA Ops:
  2.8 1.9 %copy-start = (bf16[96,128,128]{2,1,0:T(8,128)(2,1)S(1)}, bf16[96,128,128]{2,1,0:T(8,128)(2,1)}, u32[]{:S(2)}) copy-start(bf16[96,128,128]{2,1,0:T(8,128)(2,1)} %block_hbm.1) | copy-start | bytes 9437188
  4.7 2.2 %copy-start.1 = (bf16[4,512,128]{2,1,0:T(8,128)(2,1)S(1)}, bf16[4,512,128]{2,1,0:T(8,128)(2,1)}, u32[]{:S(2)}) copy-start(bf16[4,512,128]{2,1,0:T(8,128)(2,1)} %excitation.1) | copy-start | bytes 1572868
  4.7 2.2 %copy-start.2 = (f32[1,512,128]{2,1,0:T(8,128)S(1)}, f32[1,512,128]{2,1,0:T(8,128)}, u32[]{:S(2)}) copy-start(f32[1,512,128]{2,1,0:T(8,128)} %pending.1) | copy-start | bytes 786436
  4.7 2.2 %copy-start.3 = (f32[4,128,128]{2,1,0:T(8,128)S(1)}, f32[4,128,128]{2,1,0:T(8,128)}, u32[]{:S(2)}) copy-start(f32[4,128,128]{2,1,0:T(8,128)} %inverse.1) | copy-start | bytes 786436

commit v5 on v3

--- a/solution.py
+++ b/solution.py
@@ -65,7 +65,7 @@
             pltpu.SemaphoreType.DMA((slots // chunk,)),
         ],
         out_shape=[jax.ShapeDtypeStruct(shape, jnp.bfloat16)] * 2,
-        compiler_params=pltpu.CompilerParams(vmem_limit_bytes=60 * 1024 * 1024),
+        compiler_params=pltpu.CompilerParams(vmem_limit_bytes=50 * 1024 * 1024),
     )(cell, interaction)
 
 
@@ -74,7 +74,7 @@
     excitation, pending, inverse, table, high, low,
     currents, carried,
     solve_high, solve_low, own, sending, landed, handed, summed, asked, asked_scalar,
-    row_send, row_recv, lag_send, lag_recv, hand_send, hand_recv, ask_send, ask_recv, local_sem, out_sem, gate,
+    row_send, row_recv, lag_send, lag_recv, hand_send, hand_recv, ask_send, ask_recv, local_sem, out_sem,
 ):
     row = lax.axis_index("rows")
     lag = lax.axis_index("lag")
@@ -220,11 +220,6 @@
                 for entry in range(capacity):
                     block = asked_scalar[rows - away - 1, row, entry]
                     sending[step, away - 1, entry, place] = own[step][piece][block]
-            if not last:
-                @pl.when(lag == 1)
-                def _():
-                    pl.semaphore_wait(gate.at[step], 1)
-
             for away in range(1, rows):
                 row_copy(step, piece, away).start()
 
@@ -255,9 +250,6 @@
                     place = pl.ds(block * block_size, block_size)
                     value = high[place].astype(jnp.float32) + low[place].astype(jnp.float32)
                     solve_high[place], solve_low[place] = split(apply_inverse(block, value))
-            for away in range(1, rows):
-                row_copy(step, 0, away).wait_send()
-            pl.semaphore_signal(gate.at[step], inc=1, device_id=(row, 1), device_id_type=MESH)
             hand_copy(step).wait_recv()
             base = solved_part(step + 1, handed.at[step])
             keep_currents(step + 1, base - product(step, solve_high, solve_low))
@@ -285,10 +277,7 @@
                 for away in range(1, rows):
                     row_copy(step, piece, away).wait_send()
 
-            if step == steps - 1:
-                wait_rows()
-            else:
-                pl.when(lag > 0)(wait_rows)
+            wait_rows()
             out_copy(step, piece).wait()
 
             @pl.when(forwards)
@@ -348,7 +337,6 @@
             dma((rows - 1,)),
             dma((2,)),
             dma((steps, tail)),
-            pltpu.SemaphoreType.REGULAR((steps,)),
         ],
         compiler_params=pltpu.CompilerParams(
             collective_id=0, has_side_effects=True, vmem_limit_bytes=48 * 1024 * 1024

time: 57.8 us -> 53.1 us (0.919)
  local copies, waits for them, and re-layouts: 4.72 us -> 2.28 us
  Pallas kernels: 49.6 us -> 48.4 us
    unnamed x12 -> x8, local copies, waits for them, and re-layouts: 3.95 us -> 1.51 us
    pallas_call x1, Pallas kernels: 4.44 us -> 2.97 us  [collapse(): pl.pallas_call(functools.partial(collapse_kernel, chunk), in_specs=[pl.Bl...]
where the time goes in v5:
time: 53.1 us; the launch traced here: 52.9 us
  Pallas kernels  48.4 us (91%)
  local copies, waits for them, and re-layouts  2.28 us (4%)
  between operations  1.43 us (3%)
  other arithmetic  0.78 us (1%)
    pallas_call x1, Pallas kernels, per_device(): pl.pallas_call(functools.partial(window_kernel, rows, lags, steps, row_bl...  45.5 us
    pallas_call x1, Pallas kernels, collapse(): pl.pallas_call(functools.partial(collapse_kernel, chunk), in_specs=[pl.Bl...  2.97 us
    unnamed x8, local copies, waits for them, and re-layouts  1.51 us

profile of v5, /device:TPU:7, one launch (start us, length us, event | category | flops | bytes accessed | tf_op | source)
XLA Modules:
  0.0 52.9 jit_solution(2357520313695350229)
XLA Ops:
  0.6 0.0 copy-start.2
  0.6 0.0 copy-start.1
  0.7 0.0 copy-start
  1.4 0.7 %fusion.3 = s32[96]{0:T(128)S(1)} fusion(s32[96]{0:T(128)} %param.15, s32[96]{0:T(128)} %param.14, s32[96]{0:T(128)} %param.13, s32[]{:T(128)S(6)} %add.11), kind=kLoop, calls=%fused_computation.5 | loop fusion | flops 1056 | bytes 1540 | tf_op jit(solution)/shard_map/add | solution.py:54
  2.1 0.1 pad_add_fusion.cell_ref
  2.2 0.8 %copy.11 = s32[4,2]{1,0:T(4,128)S(1)} copy(s32[4,2]{0,1:T(2,128)} %bitcast.5) | data formatting | bytes 64 | tf_op jit(solution)/shard_map/squeeze | solution.py:304
  2.9 3.0 %shard_map.104 = (bf16[512,1024]{1,0:T(8,128)(2,1)S(1)}, bf16[512,1024]{1,0:T(8,128)(2,1)S(1)}) custom-call(s32[97]{0:T(128)S(1)} %pad_add_fusion.cell_ref, bf16[96,128,128]{2,1,0:T(8,128)(2,1)} %block_hbm.1), custom_call_target="tpu_custom_call" | custom-call | tf_op jit(solution)/shard_map/pallas_call | solution.py:58
  5.9 0.0 copy-done.2
  5.9 0.0 copy-done.1
  5.9 0.0 copy-done
  6.0 45.5 %shard_map.105 = (bf16[4,4,128,128]{3,2,1,0:T(8,128)(2,1)S(1)}, f32[1,512,128]{2,1,0:T(8,128)S(1)}) custom-call(bf16[4,512,128]{2,1,0:T(8,128)(2,1)S(1)} %copy-done, f32[1,512,128]{2,1,0:T(8,128)S(1)} %copy-done.1, f32[4,128,128]{2,1,0:T(8,128)S(1)} %copy-done.2, s32[8,128]{1,0:T(8,128)S(1)} %pad.4.table, bf16[512,1024]{1,0:T(8,128)(2,1)S(1)} %get-tuple-element.6.high, ...), custom_call_target="tpu_custom_call" | custom-call | tf_op jit(solution)/shard_map/pallas_call | solution.py:309
  51.4 0.8 %copy.15 = bf16[4,512,128]{2,1,0:T(8,128)(2,1)} copy(bf16[4,512,128]{2,1,0:T(8,128)(2,1)S(1)} %bitcast.4) | data formatting | bytes 1048576
  52.2 0.7 %copy.16 = f32[1,512,128]{2,1,0:T(8,128)} copy(f32[1,512,128]{2,1,0:T(8,128)S(1)} %get-tuple-element.13) | data formatting | bytes 524288
  (1 shorter events, 0.0 us)
Async XLA Ops:
  0.6 5.3 %copy-start.2 = (f32[4,128,128]{2,1,0:T(8,128)S(1)}, f32[4,128,128]{2,1,0:T(8,128)}, u32[]{:S(2)}) copy-start(f32[4,128,128]{2,1,0:T(8,128)} %inverse.1) | copy-start | bytes 786436
  0.6 5.3 %copy-start.1 = (f32[1,512,128]{2,1,0:T(8,128)S(1)}, f32[1,512,128]{2,1,0:T(8,128)}, u32[]{:S(2)}) copy-start(f32[1,512,128]{2,1,0:T(8,128)} %pending.1) | copy-start | bytes 786436
  0.7 5.3 %copy-start = (bf16[4,512,128]{2,1,0:T(8,128)(2,1)S(1)}, bf16[4,512,128]{2,1,0:T(8,128)(2,1)}, u32[]{:S(2)}) copy-start(bf16[4,512,128]{2,1,0:T(8,128)(2,1)} %excitation.1) | copy-start | bytes 1572868

commit v6 on v5

--- a/solution.py
+++ b/solution.py
@@ -186,7 +186,7 @@
     forwards = (lag > 0) & (lax.rem(lag, 2) == 0) & (lag + 1 < lags)
 
     def send_evens(step, piece):
-        for place, target in enumerate(evens):
+        for place, target in reversed(list(enumerate(evens))):
             lag_copy(step, piece, target, place + 1).start()
 
     for step in range(steps):
@@ -301,11 +301,13 @@
     high, low = collapse(
         interaction, slot_row, slot_owner, slot_pos, block_count, row_blocks, rows, capacity
     )
-    table = jnp.pad(needed[0], ((0, -rows % 8), (0, -capacity % 128)))
+    lanes = jnp.arange(capacity + -capacity % 128, dtype=jnp.int32)[None, None, :]
+    spread = sum(jnp.where(lanes == entry, needed[:, :, entry : entry + 1], 0) for entry in range(capacity))
+    table = jnp.pad(spread, ((0, 0), (0, -rows % 8), (0, 0)))[0]
     vmem = pl.BlockSpec(memory_space=pltpu.VMEM)
     dma = pltpu.SemaphoreType.DMA
     evens = len(range(2, lags, 2))
-    tail = 2 if block_size % 32 == 0 else 1
+    tail = 4 if block_size % 64 == 0 else 1
     return pl.pallas_call(
         functools.partial(window_kernel, rows, lags, steps, row_blocks, capacity),
         out_shape=[

time: 53.1 us -> 54.7 us (1.030)
  the two profiles are of different devices: /device:TPU:7 before, /device:TPU:3 now
where the time goes in v6:
time: 54.7 us; the launch traced here: 54.3 us
  Pallas kernels  49.7 us (91%)
  local copies, waits for them, and re-layouts  2.27 us (4%)
  between operations  1.43 us (3%)
  other arithmetic  0.86 us (2%)
    pallas_call x1, Pallas kernels, per_device(): pl.pallas_call(functools.partial(window_kernel, rows, lags, steps, row_bl...  46.8 us
    pallas_call x1, Pallas kernels, collapse(): pl.pallas_call(functools.partial(collapse_kernel, chunk), in_specs=[pl.Bl...  2.97 us
    unnamed x8, local copies, waits for them, and re-layouts  1.51 us

profile of v6, /device:TPU:3, one launch (start us, length us, event | category | flops | bytes accessed | tf_op | source)
XLA Modules:
  0.0 54.3 jit_solution(146949607063303126)
XLA Ops:
  0.6 0.0 copy-start.2
  0.6 0.0 copy-start.1
  0.7 0.0 copy-start
  1.4 0.7 %fusion.3 = s32[96]{0:T(128)S(1)} fusion(s32[96]{0:T(128)} %param.15, s32[96]{0:T(128)} %param.14, s32[96]{0:T(128)} %param.13, s32[]{:T(128)S(6)} %add.23), kind=kLoop, calls=%fused_computation.7 | loop fusion | flops 1056 | bytes 1540 | tf_op jit(solution)/shard_map/add | solution.py:54
  2.1 0.1 pad_add_fusion.cell_ref
  2.2 0.8 %slice_bitcast_fusion.1 = (s32[4]{0:T(128)S(1)}, s32[4]{0:T(128)S(1)}) fusion(s32[1,4,2]{1,2,0:T(2,128)} %param.16), kind=kLoop, calls=%fused_computation.11 | loop fusion | bytes 64 | tf_op jit(solution)/shard_map/jit(_where)/broadcast_in_dim | solution.py:305
  2.9 0.1 select_add_fusion
  3.0 3.0 %shard_map.104 = (bf16[512,1024]{1,0:T(8,128)(2,1)S(1)}, bf16[512,1024]{1,0:T(8,128)(2,1)S(1)}) custom-call(s32[97]{0:T(128)S(1)} %pad_add_fusion.cell_ref, bf16[96,128,128]{2,1,0:T(8,128)(2,1)} %block_hbm.1), custom_call_target="tpu_custom_call" | custom-call | tf_op jit(solution)/shard_map/pallas_call | solution.py:58
  6.0 0.0 copy-done.2
  6.0 0.0 copy-done.1
  6.0 0.0 copy-done
  6.0 46.8 %shard_map.105 = (bf16[4,4,128,128]{3,2,1,0:T(8,128)(2,1)S(1)}, f32[1,512,128]{2,1,0:T(8,128)S(1)}) custom-call(bf16[4,512,128]{2,1,0:T(8,128)(2,1)S(1)} %copy-done, f32[1,512,128]{2,1,0:T(8,128)S(1)} %copy-done.1, f32[4,128,128]{2,1,0:T(8,128)S(1)} %copy-done.2, s32[8,128]{1,0:T(8,128)S(1)} %pad_bitcast_fusion.table, ...), custom_call_target="tpu_custom_call" | custom-call | tf_op jit(solution)/shard_map/pallas_call | solution.py:311
  52.8 0.8 %copy.14 = bf16[4,512,128]{2,1,0:T(8,128)(2,1)} copy(bf16[4,512,128]{2,1,0:T(8,128)(2,1)S(1)} %bitcast.9) | data formatting | bytes 1048576
  53.6 0.7 %copy.15 = f32[1,512,128]{2,1,0:T(8,128)} copy(f32[1,512,128]{2,1,0:T(8,128)S(1)} %get-tuple-element.17) | data formatting | bytes 524288
  (2 shorter events, 0.0 us)
Async XLA Ops:
  0.6 5.4 %copy-start.2 = (f32[4,128,128]{2,1,0:T(8,128)S(1)}, f32[4,128,128]{2,1,0:T(8,128)}, u32[]{:S(2)}) copy-start(f32[4,128,128]{2,1,0:T(8,128)} %inverse.1) | copy-start | bytes 786436
  0.6 5.4 %copy-start.1 = (f32[1,512,128]{2,1,0:T(8,128)S(1)}, f32[1,512,128]{2,1,0:T(8,128)}, u32[]{:S(2)}) copy-start(f32[1,512,128]{2,1,0:T(8,128)} %pending.1) | copy-start | bytes 786436
  0.7 5.4 %copy-start = (bf16[4,512,128]{2,1,0:T(8,128)(2,1)S(1)}, bf16[4,512,128]{2,1,0:T(8,128)(2,1)}, u32[]{:S(2)}) copy-start(bf16[4,512,128]{2,1,0:T(8,128)(2,1)} %excitation.1) | copy-start | bytes 1572868

commit v7 on v5

--- a/solution.py
+++ b/solution.py
@@ -182,7 +182,8 @@
         handed[...] = jnp.zeros_like(handed)
 
     to_scalar = pltpu.make_async_copy(asked, asked_scalar.at[pl.ds(0, rows - 1)], local_sem.at[1])
-    evens = list(range(2, lags, 2))
+    evens = [target for target in range(2, lags, 2) if target == 2 or target % 4 == 0]
+    relays = (lag > 0) & (lax.rem(lag, 4) == 0) & (lag + 2 < lags)
     forwards = (lag > 0) & (lax.rem(lag, 2) == 0) & (lag + 1 < lags)
 
     def send_evens(step, piece):
@@ -210,6 +211,10 @@
                 to_scalar.start()
                 own_table.wait()
                 to_scalar.wait()
+
+            @pl.when(relays)
+            def _():
+                lag_copy(step, piece, lag + 2, 1).start()
 
             @pl.when(forwards)
             def _():
@@ -279,6 +284,10 @@
 
             wait_rows()
             out_copy(step, piece).wait()
+
+            @pl.when(relays)
+            def _():
+                lag_copy(step, piece, lag + 2, 1).wait_send()
 
             @pl.when(forwards)
             def _():

time: 53.1 us -> 58.7 us (1.11)
  Pallas kernels: 48.4 us -> 54.1 us
    pallas_call x1, Pallas kernels: 45.5 us -> 51.2 us  [per_device(): pl.pallas_call(functools.partial(window_kernel, rows, lags, steps, row_bl...]
where the time goes in v7:
time: 58.7 us; the launch traced here: 58.6 us
  Pallas kernels  54.1 us (92%)
  local copies, waits for them, and re-layouts  2.28 us (4%)
  between operations  1.43 us (2%)
  other arithmetic  0.78 us (1%)
    pallas_call x1, Pallas kernels, per_device(): pl.pallas_call(functools.partial(window_kernel, rows, lags, steps, row_bl...  51.2 us
    pallas_call x1, Pallas kernels, collapse(): pl.pallas_call(functools.partial(collapse_kernel, chunk), in_specs=[pl.Bl...  2.97 us
    unnamed x8, local copies, waits for them, and re-layouts  1.51 us

profile of v7, /device:TPU:7, one launch (start us, length us, event | category | flops | bytes accessed | tf_op | source)
XLA Modules:
  0.0 58.6 jit_solution(8021698254317435791)
XLA Ops:
  0.6 0.0 copy-start.2
  0.6 0.0 copy-start.1
  0.7 0.0 copy-start
  1.4 0.7 %fusion.3 = s32[96]{0:T(128)S(1)} fusion(s32[96]{0:T(128)} %param.15, s32[96]{0:T(128)} %param.14, s32[96]{0:T(128)} %param.13, s32[]{:T(128)S(6)} %add.11), kind=kLoop, calls=%fused_computation.5 | loop fusion | flops 1056 | bytes 1540 | tf_op jit(solution)/shard_map/add | solution.py:54
  2.1 0.1 pad_add_fusion.cell_ref
  2.2 0.8 %copy.11 = s32[4,2]{1,0:T(4,128)S(1)} copy(s32[4,2]{0,1:T(2,128)} %bitcast.5) | data formatting | bytes 64 | tf_op jit(solution)/shard_map/squeeze | solution.py:313
  2.9 3.0 %shard_map.104 = (bf16[512,1024]{1,0:T(8,128)(2,1)S(1)}, bf16[512,1024]{1,0:T(8,128)(2,1)S(1)}) custom-call(s32[97]{0:T(128)S(1)} %pad_add_fusion.cell_ref, bf16[96,128,128]{2,1,0:T(8,128)(2,1)} %block_hbm.1), custom_call_target="tpu_custom_call" | custom-call | tf_op jit(solution)/shard_map/pallas_call | solution.py:58
  5.9 0.0 copy-done.2
  5.9 0.0 copy-done.1
  5.9 0.0 copy-done
  6.0 51.2 %shard_map.105 = (bf16[4,4,128,128]{3,2,1,0:T(8,128)(2,1)S(1)}, f32[1,512,128]{2,1,0:T(8,128)S(1)}) custom-call(bf16[4,512,128]{2,1,0:T(8,128)(2,1)S(1)} %copy-done, f32[1,512,128]{2,1,0:T(8,128)S(1)} %copy-done.1, f32[4,128,128]{2,1,0:T(8,128)S(1)} %copy-done.2, s32[8,128]{1,0:T(8,128)S(1)} %pad.4.table, bf16[512,1024]{1,0:T(8,128)(2,1)S(1)} %get-tuple-element.6.high, ...), custom_call_target="tpu_custom_call" | custom-call | tf_op jit(solution)/shard_map/pallas_call | solution.py:318
  57.1 0.8 %copy.15 = bf16[4,512,128]{2,1,0:T(8,128)(2,1)} copy(bf16[4,512,128]{2,1,0:T(8,128)(2,1)S(1)} %bitcast.4) | data formatting | bytes 1048576
  57.9 0.7 %copy.16 = f32[1,512,128]{2,1,0:T(8,128)} copy(f32[1,512,128]{2,1,0:T(8,128)S(1)} %get-tuple-element.13) | data formatting | bytes 524288
  (1 shorter events, 0.0 us)
Async XLA Ops:
  0.6 5.3 %copy-start.2 = (f32[4,128,128]{2,1,0:T(8,128)S(1)}, f32[4,128,128]{2,1,0:T(8,128)}, u32[]{:S(2)}) copy-start(f32[4,128,128]{2,1,0:T(8,128)} %inverse.1) | copy-start | bytes 786436
  0.6 5.3 %copy-start.1 = (f32[1,512,128]{2,1,0:T(8,128)S(1)}, f32[1,512,128]{2,1,0:T(8,128)}, u32[]{:S(2)}) copy-start(f32[1,512,128]{2,1,0:T(8,128)} %pending.1) | copy-start | bytes 786436
  0.7 5.3 %copy-start = (bf16[4,512,128]{2,1,0:T(8,128)(2,1)S(1)}, bf16[4,512,128]{2,1,0:T(8,128)(2,1)}, u32[]{:S(2)}) copy-start(bf16[4,512,128]{2,1,0:T(8,128)(2,1)} %excitation.1) | copy-start | bytes 1572868
